TPU v7x, 128 devices: a whole 4x4x4 slice. The times are simulated.
128 devices in a mesh: section: 2 (over core), seq: 4 (over z), dp: 16 (over y, x).
Axes of the slice: x: 4, y: 4, z: 4, core: 2. Of those that a mesh axis runs over, the one named last changes fastest.
Arguments:
- inputs: bfloat16 [32, 1024, 768], P('dp', 'seq'), may hold values from -6 to 6
- cotangent: bfloat16 [32, 1024, 768], P('dp', 'seq'), may hold values from -6 to 6
- w_qkv: bfloat16 [2, 768, 2304], P('section', 'dp'), may hold values from -0.21875 to 0.21875
- w_out: bfloat16 [2, 768, 768], P('section', 'dp'), may hold values from -1.25 to 1.25
- w_fc: bfloat16 [2, 768, 3072], P('section', 'dp'), may hold values from -0.21875 to 0.21875
- w_proj: bfloat16 [2, 3072, 768], P('section', 'dp'), may hold values from -0.109375 to 0.109375
- gains: bfloat16 [2, 2, 768], P('section', None, 'dp'), may hold values from 0.099609375 to 1.8984375
- biases: bfloat16 [2, 6, 768], P('section', None, 'dp'), may hold values from -3 to 3
- fc_bias: bfloat16 [2, 3072], P('section', 'dp'), may hold values from -3 to 3
Outputs:
- section_out: bfloat16 [2, 32, 1024, 768], P('section', 'dp', 'seq')
- in_grad: bfloat16 [2, 32, 1024, 768], P('section', 'dp', 'seq')
- grad_qkv: float32 [2, 768, 2304], P('section', 'dp')
- grad_out: float32 [2, 768, 768], P('section', 'dp')
- grad_fc: float32 [2, 768, 3072], P('section', 'dp')
- grad_proj: float32 [2, 3072, 768], P('section', 'dp')
- grad_gains: float32 [2, 2, 768], P('section', None, 'dp')
- grad_biases: float32 [2, 6, 768], P('section', None, 'dp')
- grad_fc_bias: float32 [2, 3072], P('section', 'dp')
All inputs are finite; a program needn't handle non-finite values.
Results may differ from a plain program's by a relative error of at most 0.019.
Values may be sent and summed in bfloat16 or wider, within the bound.
A program may use at most 256 MiB of HBM per device.

v0:
```python
import jax
import jax.numpy as jnp
from jax import lax
from jax.sharding import PartitionSpec as P

HEAD = 64


epsilon = 1e-05


def for_sending(x):
    return jax.tree.map(lambda a: a.astype(jnp.bfloat16) if a.dtype == jnp.float32 else a, x)


def passed_along(block, axis, distance):
    devices = range(lax.axis_size(axis))
    route = [(i - distance, i) for i in devices if i - distance in devices]
    return lax.ppermute(block, axis, route)


def layer_norm(stream, gain, shift):
    centre = stream - jnp.mean(stream, axis=-1, keepdims=True)
    spread = jnp.mean(centre * centre, axis=-1, keepdims=True)
    return centre * lax.rsqrt(spread + epsilon) * gain + shift


def gelu_tanh(value):
    return jax.nn.gelu(value, approximate=True)


def guarded(valid, work, *operands):

    def skipped(*inner):
        return jax.tree.map(jnp.zeros_like, work(*inner))

    return lax.cond(valid, work, skipped, *operands)


def body(inputs, cotangent, w_qkv, w_out, w_fc, w_proj, gains, biases, fc_bias):
    section = lax.axis_index("section")
    seq_count = lax.axis_size("seq")
    gathered = (
        lax.all_gather(w_qkv, "dp", axis=1, tiled=True),
        lax.all_gather(w_out, "dp", axis=1, tiled=True),
        lax.all_gather(w_fc, "dp", axis=1, tiled=True),
        lax.all_gather(w_proj, "dp", axis=1, tiled=True),
        lax.all_gather(gains, "dp", axis=2, tiled=True),
        lax.all_gather(biases, "dp", axis=2, tiled=True),
        lax.all_gather(fc_bias, "dp", axis=1, tiled=True),
    )
    w_in = gathered[0][0]
    w_mix = gathered[1][0]
    w_up = gathered[2][0]
    w_down = gathered[3][0]
    gain_rows = gathered[4][0].astype(jnp.float32)
    shift_rows = gathered[5][0].astype(jnp.float32)
    up_shift = gathered[6][0].astype(jnp.float32)
    micro, tokens, width = inputs.shape
    hidden = w_up.shape[1]
    length = tokens * seq_count
    local_width = width // seq_count
    local_heads = local_width // HEAD
    rows = min(512, length)
    scale = HEAD ** (-0.5)
    qkv_shift = jnp.concatenate([shift_rows[1], jnp.zeros_like(shift_rows[1]), shift_rows[2]])

    def front(entry):
        stream = entry.astype(jnp.float32)
        normed = layer_norm(stream, gain_rows[0], shift_rows[0]).astype(jnp.bfloat16)
        packed = jnp.dot(normed, w_in, preferred_element_type=jnp.float32) + qkv_shift
        return (normed, packed.astype(jnp.bfloat16).reshape(tokens, 3, width))

    def split_heads(heads):
        return tuple((heads[:, part].reshape(length, local_heads, HEAD) for part in range(3)))

    def masked_scores(block_q, keys_in, start, stop):
        scores = (
            jnp.einsum("qhd,khd->hqk", block_q, keys_in[:stop], preferred_element_type=jnp.float32)
            * scale
        )
        query_pos = start + jnp.arange(rows)[:, None]
        key_pos = jnp.arange(stop)[None, :]
        return jnp.where(key_pos <= query_pos, scores, -1e30)

    def attend(heads):
        queries, keys_in, values_in = split_heads(heads)
        pieces = []
        totals = []
        for index in range(length // rows):
            start = index * rows
            stop = start + rows
            scores = masked_scores(queries[start:stop], keys_in, start, stop)
            peak = jnp.max(scores, axis=-1, keepdims=True)
            total = peak + jnp.log(jnp.sum(jnp.exp(scores - peak), axis=-1, keepdims=True))
            weights = jnp.exp(scores - total).astype(jnp.bfloat16)
            mixed = jnp.einsum(
                "hqk,khd->qhd", weights, values_in[:stop], preferred_element_type=jnp.float32
            )
            pieces.append(mixed.reshape(rows, local_width).astype(jnp.bfloat16))
            totals.append(total[..., 0])
        return (jnp.concatenate(pieces, 0), jnp.concatenate(totals, 1))

    def rear(entry, mixed_tok):
        stream = entry.astype(jnp.float32)
        middle = stream + (
            jnp.dot(mixed_tok, w_mix, preferred_element_type=jnp.float32) + shift_rows[3]
        )
        normed2 = layer_norm(middle, gain_rows[1], shift_rows[4]).astype(jnp.bfloat16)
        pre_act = jnp.dot(normed2, w_up, preferred_element_type=jnp.float32) + up_shift
        active = gelu_tanh(pre_act).astype(jnp.bfloat16)
        result = middle + (
            jnp.dot(active, w_down, preferred_element_type=jnp.float32) + shift_rows[5]
        )
        return (middle, normed2, pre_act, active, result.astype(jnp.bfloat16))

    padded_in = jnp.concatenate([inputs, jnp.zeros_like(inputs[:1])], 0)

    def forward_tick(received, tick):
        fresh = lax.dynamic_index_in_dim(padded_in, tick, 0, keepdims=False)
        entry = jnp.where(section == 0, fresh, received)
        valid = (tick >= section) & (tick < section + micro)
        normed, packed = guarded(valid, front, entry)
        heads = lax.all_to_all(packed, "seq", split_axis=2, concat_axis=0, tiled=True)
        mixed_heads, totals = guarded(valid, attend, heads)
        mixed_tok = lax.all_to_all(
            for_sending(mixed_heads), "seq", split_axis=0, concat_axis=1, tiled=True
        ).astype(mixed_heads.dtype)
        middle, normed2, pre_act, active, result = guarded(valid, rear, entry, mixed_tok)
        sent = passed_along(result, "section", 1)
        return (
            sent,
            (entry, normed, heads, totals, mixed_tok, middle, normed2, pre_act, active, result),
        )

    ticks = jnp.arange(micro + 1, dtype=jnp.int32)
    _, kept = lax.scan(forward_tick, jnp.zeros_like(inputs[0]), ticks)
    section_out = lax.dynamic_slice_in_dim(kept[9], section, micro, 0)[None]

    def rear_back(grad_top, middle, normed2, pre_act, active, mixed_tok):
        grad_low = grad_top.astype(jnp.bfloat16)
        grad_down = jnp.einsum("tf,td->fd", active, grad_low, preferred_element_type=jnp.float32)
        grad_down_shift = jnp.sum(grad_top, 0)
        grad_act = jnp.dot(grad_low, w_down.T, preferred_element_type=jnp.float32)
        _, gelu_pull = jax.vjp(gelu_tanh, pre_act)
        grad_pre = gelu_pull(grad_act)[0].astype(jnp.bfloat16)
        grad_up_shift = jnp.sum(grad_pre.astype(jnp.float32), 0)
        grad_up = jnp.einsum("td,tf->df", normed2, grad_pre, preferred_element_type=jnp.float32)
        grad_norm = jnp.dot(grad_pre, w_up.T, preferred_element_type=jnp.float32)
        _, norm_pull = jax.vjp(layer_norm, middle, gain_rows[1], shift_rows[4])
        grad_inner, grad_gain2, grad_shift2 = norm_pull(grad_norm)
        grad_middle = grad_top + grad_inner
        middle_low = grad_middle.astype(jnp.bfloat16)
        grad_mix = jnp.einsum(
            "td,te->de", mixed_tok, middle_low, preferred_element_type=jnp.float32
        )
        grad_mix_shift = jnp.sum(grad_middle, 0)
        grad_mixed = jnp.dot(middle_low, w_mix.T, preferred_element_type=jnp.float32).astype(
            jnp.bfloat16
        )
        return (
            grad_mixed,
            grad_middle,
            (
                grad_down,
                grad_down_shift,
                grad_up,
                grad_up_shift,
                grad_mix,
                grad_mix_shift,
                grad_gain2,
                grad_shift2,
            ),
        )

    def attend_back(heads, totals, grad_mixed):
        queries, keys_in, values_in = split_heads(heads)
        grad_top = grad_mixed.reshape(length, local_heads, HEAD)
        grad_queries = []
        grad_keys = jnp.zeros((length, local_heads, HEAD), jnp.float32)
        grad_values = jnp.zeros((length, local_heads, HEAD), jnp.float32)
        for index in range(length // rows):
            start = index * rows
            stop = start + rows
            scores = masked_scores(queries[start:stop], keys_in, start, stop)
            weights = jnp.exp(scores - totals[:, start:stop, None])
            grad_weights = jnp.einsum(
                "qhd,khd->hqk",
                grad_top[start:stop],
                values_in[:stop],
                preferred_element_type=jnp.float32,
            )
            inner = jnp.sum(weights * grad_weights, axis=-1, keepdims=True)
            grad_scores = (weights * (grad_weights - inner)).astype(jnp.bfloat16)
            grad_queries.append(
                jnp.einsum(
                    "hqk,khd->qhd", grad_scores, keys_in[:stop], preferred_element_type=jnp.float32
                )
                * scale
            )
            margin = ((0, length - stop), (0, 0), (0, 0))
            key_part = (
                jnp.einsum(
                    "hqk,qhd->khd",
                    grad_scores,
                    queries[start:stop],
                    preferred_element_type=jnp.float32,
                )
                * scale
            )
            value_part = jnp.einsum(
                "hqk,qhd->khd",
                weights.astype(jnp.bfloat16),
                grad_top[start:stop],
                preferred_element_type=jnp.float32,
            )
            grad_keys = grad_keys + jnp.pad(key_part, margin)
            grad_values = grad_values + jnp.pad(value_part, margin)
        stacked = jnp.stack([jnp.concatenate(grad_queries, 0), grad_keys, grad_values], 1)
        return stacked.reshape(length, 3, local_width).astype(jnp.bfloat16)

    def front_back(grad_packed, grad_middle, entry, normed):
        flat = grad_packed.reshape(tokens, 3 * width)
        grad_in = jnp.einsum("td,te->de", normed, flat, preferred_element_type=jnp.float32)
        widened = flat.astype(jnp.float32)
        grad_query_shift = jnp.sum(widened[:, :width], 0)
        grad_value_shift = jnp.sum(widened[:, 2 * width :], 0)
        grad_norm = jnp.dot(flat, w_in.T, preferred_element_type=jnp.float32)
        _, norm_pull = jax.vjp(layer_norm, entry.astype(jnp.float32), gain_rows[0], shift_rows[0])
        grad_entry, grad_gain1, grad_shift1 = norm_pull(grad_norm)
        return (
            grad_middle + grad_entry,
            (grad_in, grad_query_shift, grad_value_shift, grad_gain1, grad_shift1),
        )

    padded_cot = jnp.concatenate([cotangent, jnp.zeros_like(cotangent[:1])], 0)

    def backward_tick(carry, tick):
        received, sums = carry
        index = tick - 1 + section
        valid = (index >= 0) & (index < micro)
        slot = jnp.clip(index + section, 0, micro)
        picked = tuple((lax.dynamic_index_in_dim(item, slot, 0, keepdims=False) for item in kept))
        entry, normed, heads, totals, mixed_tok, middle, normed2, pre_act, active = picked[:9]
        outside = lax.dynamic_index_in_dim(padded_cot, tick, 0, keepdims=False)
        grad_top = jnp.where(section == 1, outside, received).astype(jnp.float32)
        grad_mixed_tok, grad_middle, rear_grads = guarded(
            valid, rear_back, grad_top, middle, normed2, pre_act, active, mixed_tok
        )
        grad_mixed = lax.all_to_all(grad_mixed_tok, "seq", split_axis=1, concat_axis=0, tiled=True)
        grad_heads = guarded(valid, attend_back, heads, totals, grad_mixed)
        grad_packed = lax.all_to_all(grad_heads, "seq", split_axis=0, concat_axis=2, tiled=True)
        grad_entry, front_grads = guarded(
            valid, front_back, grad_packed, grad_middle, entry, normed
        )
        grad_low = grad_entry.astype(jnp.bfloat16)
        passed = passed_along(grad_low, "section", -1)
        terms = (
            front_grads[0],
            rear_grads[4],
            rear_grads[2],
            rear_grads[0],
            jnp.stack([front_grads[3], rear_grads[6]]),
            jnp.stack(
                [
                    front_grads[4],
                    front_grads[1],
                    front_grads[2],
                    rear_grads[5],
                    rear_grads[7],
                    rear_grads[1],
                ]
            ),
            rear_grads[3],
        )
        sums = tuple((total + term for total, term in zip(sums, terms)))
        return ((passed, sums), grad_low)

    zero_sums = (
        jnp.zeros((width, 3 * width), jnp.float32),
        jnp.zeros((width, width), jnp.float32),
        jnp.zeros((width, hidden), jnp.float32),
        jnp.zeros((hidden, width), jnp.float32),
        jnp.zeros((2, width), jnp.float32),
        jnp.zeros((6, width), jnp.float32),
        jnp.zeros((hidden,), jnp.float32),
    )
    (_, sums), grads_in = lax.scan(backward_tick, (jnp.zeros_like(inputs[0]), zero_sums), ticks)
    in_grad = lax.dynamic_slice_in_dim(grads_in, 1 - section, micro, 0)[None]
    lifted = tuple((item[None] for item in sums))
    parts = (
        lax.psum_scatter(
            lifted[0].astype(jnp.bfloat16), "dp", scatter_dimension=1, tiled=True
        ).astype(jnp.float32),
        lax.psum_scatter(
            lifted[1].astype(jnp.bfloat16), "dp", scatter_dimension=1, tiled=True
        ).astype(jnp.float32),
        lax.psum_scatter(
            lifted[2].astype(jnp.bfloat16), "dp", scatter_dimension=1, tiled=True
        ).astype(jnp.float32),
        lax.psum_scatter(
            lifted[3].astype(jnp.bfloat16), "dp", scatter_dimension=1, tiled=True
        ).astype(jnp.float32),
        lax.psum_scatter(
            lifted[4].astype(jnp.bfloat16), "dp", scatter_dimension=2, tiled=True
        ).astype(jnp.float32),
        lax.psum_scatter(
            lifted[5].astype(jnp.bfloat16), "dp", scatter_dimension=2, tiled=True
        ).astype(jnp.float32),
        lax.psum_scatter(
            lifted[6].astype(jnp.bfloat16), "dp", scatter_dimension=1, tiled=True
        ).astype(jnp.float32),
    )
    grads = jax.tree.map(lambda part: part.astype(jnp.float32), lax.psum(for_sending(parts), "seq"))
    return (
        section_out,
        in_grad,
        grads[0],
        grads[1],
        grads[2],
        grads[3],
        grads[4],
        grads[5],
        grads[6],
    )


def solution(mesh):
    in_specs = (
        P("dp", "seq", None),
        P("dp", "seq", None),
        P("section", "dp", None),
        P("section", "dp", None),
        P("section", "dp", None),
        P("section", "dp", None),
        P("section", None, "dp"),
        P("section", None, "dp"),
        P("section", "dp"),
    )
    out_specs = (
        P("section", "dp", "seq", None),
        P("section", "dp", "seq", None),
        P("section", "dp", None),
        P("section", "dp", None),
        P("section", "dp", None),
        P("section", "dp", None),
        P("section", None, "dp"),
        P("section", None, "dp"),
        P("section", "dp"),
    )
    return jax.shard_map(body, mesh=mesh, in_specs=in_specs, out_specs=out_specs, check_vma=False)
```

profile of v0, /device:TPU:1, one launch (start us, length us, event | category | flops | bytes accessed | tf_op | source)
XLA Modules:
  0.0 1321.3 jit_solution(7681521563416561607)
XLA Ops:
  13.1 34.9 %all-reduce.4 = bf16[3072]{0:T(1024)(128)(2,1)S(1)} all-reduce(bf16[3072]{0:T(1024)(128)(2,1)S(1)} %dynamic-update-slice), channel_id=1, replica_groups=mesh['section'=2,'seq'=4,'dp'=16] {'dp'}, use_global_device_ids=true, to_apply=%add.4 | all-reduce | flops 3072 | bytes 12288
  50.1 16.3 %all_gather.22 = bf16[1,6,768]{1,0,2:T(2,128)(2,1)S(1)} all-gather(bf16[1,6,48]{1,0,2:T(2,128)(2,1)S(1)} %copy.93), channel_id=1, replica_groups=mesh['section'=2,'seq'=4,'dp'=16] {'dp'}, dimensions={2}, use_global_device_ids=true | all-gather | bytes 9792 | tf_op jit(solution)/shard_map/all_gather | solution.py:49
  67.6 19.4 %all_gather.21 = bf16[1,2,768]{1,0,2:T(2,128)(2,1)S(1)} all-gather(bf16[1,2,48]{1,0,2:T(2,128)(2,1)S(1)} %copy.92), channel_id=1, replica_groups=mesh['section'=2,'seq'=4,'dp'=16] {'dp'}, dimensions={2}, use_global_device_ids=true | all-gather | bytes 3264 | tf_op jit(solution)/shard_map/all_gather | solution.py:48
  96.2 11.4 all-gather.5.cloned.1.call-done
  107.6 55.7 %all-gather.9.cloned.1.call-done = bf16[1,768,3072]{2,1,0:T(8,128)(2,1)} async-done(((bf16[1,48,3072]{2,1,0:T(8,128)(2,1)}), bf16[1,768,3072]{2,1,0:T(8,128)(2,1)}) %all-gather.9.cloned.1.call-update) | async-done | bytes 4718608 | tf_op jit(solution)/shard_map/all_gather | solution.py:46
  163.3 55.6 %all-gather.11.cloned.1.call-done = bf16[1,3072,768]{2,1,0:T(8,128)(2,1)} async-done(((bf16[1,192,768]{2,1,0:T(8,128)(2,1)}), bf16[1,3072,768]{2,1,0:T(8,128)(2,1)}) %all-gather.11.cloned.1.call-update) | async-done | bytes 4718608 | tf_op jit(solution)/shard_map/all_gather | solution.py:47
  225.2 241.7 %while.60 = (s32[]{:T(128)}, bf16[256,768]{1,0:T(8,128)(2,1)}, bf16[3,256,768]{2,1,0:T(8,128)(2,1)}, bf16[3,256,768]{2,1,0:T(8,128)(2,1)}, bf16[3,1024,3,192]{1,...) while((s32[]{:T(128)}, bf16[256,768]{1,0:T(8,128)(2,1)}, ...), condition=%wide.region_15.16_spmd, body=%wide.region_0.15_spmd.sunk | while | flops 4279370752 | bytes 133605784 | solution.py:137
  237.8 14.5 %all-to-all-done = bf16[256,3,768]{0,1,2:T(4,128)(2,1)S(1)} async-done(((bf16[256,3,768]{0,1,2:T(4,128)(2,1)}), bf16[256,3,768]{0,1,2:T(4,128)(2,1)S(1)}, u32[]{:S(2)}, u32[]{:S(2)}) %all-to-all-start) | async-done | bytes 1179680 | tf_op jit(solution)/shard_map/while/body/eval_jaxpr/all_to_all | solution.py:124
  276.4 25.7 %collective-permute-done = bf16[256,768]{1,0:T(8,128)(2,1)} collective-permute-done((bf16[256,768]{1,0:T(8,128)(2,1)}, bf16[256,768]{1,0:T(8,128)(2,1)}, u32[]{:S(2)}, u32[]{:S(2)}) %collective-permute-start) | collective-permute-done | bytes 393248 | tf_op jit(solution)/shard_map/while/body/eval_jaxpr/ppermute | solution.py:19
  319.0 13.5 %all-to-all-done = bf16[256,3,768]{0,1,2:T(4,128)(2,1)S(1)} async-done(((bf16[256,3,768]{0,1,2:T(4,128)(2,1)}), bf16[256,3,768]{0,1,2:T(4,128)(2,1)S(1)}, u32[]{:S(2)}, u32[]{:S(2)}) %all-to-all-start) | async-done | bytes 1179680 | tf_op jit(solution)/shard_map/while/body/eval_jaxpr/all_to_all | solution.py:124
  353.3 17.8 %conditional.17 = (bf16[256,768]{1,0:T(8,128)(2,1)}, bf16[1,256,768]{2,1,0:T(8,128)(2,1)S(1)}, f32[1,256,768]{2,1,0:T(8,128)S(1)}, bf16[1,256,768]{2,1,0:T(8,128...) conditional(s32[]{:T(128)} %convert_element_type.374, () %tuple.223, ...), branch_computations={%region_11.11_spmd, %region_12.14_spmd} | conditional | flops 2736783616 | bytes 48481460 | solution.py:37
  400.1 18.9 %all-to-all-done = bf16[256,3,768]{0,1,2:T(4,128)(2,1)S(1)} async-done(((bf16[256,3,768]{0,1,2:T(4,128)(2,1)}), bf16[256,3,768]{0,1,2:T(4,128)(2,1)S(1)}, u32[]{:S(2)}, u32[]{:S(2)}) %all-to-all-start) | async-done | bytes 1179680 | tf_op jit(solution)/shard_map/while/body/eval_jaxpr/all_to_all | solution.py:124
  439.9 17.8 %conditional.17 = (bf16[256,768]{1,0:T(8,128)(2,1)}, bf16[1,256,768]{2,1,0:T(8,128)(2,1)S(1)}, f32[1,256,768]{2,1,0:T(8,128)S(1)}, bf16[1,256,768]{2,1,0:T(8,128...) conditional(s32[]{:T(128)} %convert_element_type.374, () %tuple.223, ...), branch_computations={%region_11.11_spmd, %region_12.14_spmd} | conditional | flops 2736783616 | bytes 48481460 | solution.py:37
  468.6 401.9 %while.61 = (s32[]{:T(128)}, bf16[256,768]{1,0:T(8,128)(2,1)S(1)}, f32[768,2304]{1,0:T(8,128)}, f32[768,768]{1,0:T(8,128)}, f32[768,3072]{1,0:T(8,128)}, /*index...) while((s32[]{:T(128)}, bf16[256,768]{1,0:T(8,128)(2,1)S(1)}, ...), condition=%wide.region_42.43_spmd.clone, body=%wide.region_16.42_spmd.clone.sunk | while | flops 8837049344 | bytes 306952384 | solution.py:288
  494.3 30.1 %conditional.18 = (bf16[256,768]{1,0:T(8,128)(2,1)S(1)}, f32[256,768]{1,0:T(8,128)}, f32[3072,768]{1,0:T(8,128)}, f32[768,3072]{1,0:T(8,128)}, f32[3072]{0:T(102...) conditional(s32[]{:T(128)} %convert_element_type.376, ...), branch_computations={%region_17.17_spmd, %region_18.27_spmd} | conditional | flops 5458620416 | bytes 86591160 | solution.py:37
  539.1 21.1 %conditional.19 = (bf16[1024,3,192]{0,2,1:T(8,128)(2,1)S(1)}) conditional(s32[]{:T(128)} %convert_element_type.376, () %tuple.230, (bf16[3,1024,3,192]{1,3,2,0:T(8,128)(2,1)}, s32[]{:T(128)}, f32[3,3,1024]{2,1,0:T(4,128)}, bf16[4,256,192]{1,2,0:T(8,128)(2,1)S(1)}) %tuple.278), branch_computations={%region_28.28_spmd, %region_29.31_spmd} | conditional | flops 1544844800 | bytes 92180552 | solution.py:37
  586.6 15.7 %conditional.20 = (f32[768,2304]{1,0:T(8,128)}, bf16[256,768]{1,0:T(8,128)(2,1)}, bf16[1,256,768]{2,1,0:T(8,128)(2,1)S(1)}, f32[1,768]{1,0:T(1,128)S(1)}, f32[1,...) conditional(s32[]{:T(128)} %convert_element_type.376, () %tuple.229, ...), branch_computations={%region_32.32_spmd, %region_33.41_spmd} | conditional | flops 1819015424 | bytes 26811976 | solution.py:37
  618.1 30.1 %conditional.18 = (bf16[256,768]{1,0:T(8,128)(2,1)S(1)}, f32[256,768]{1,0:T(8,128)}, f32[3072,768]{1,0:T(8,128)}, f32[768,3072]{1,0:T(8,128)}, f32[3072]{0:T(102...) conditional(s32[]{:T(128)} %convert_element_type.376, ...), branch_computations={%region_17.17_spmd, %region_18.27_spmd} | conditional | flops 5458620416 | bytes 86591160 | solution.py:37
  652.6 13.0 select_add_fusion.14
  665.6 21.1 %conditional.19 = (bf16[1024,3,192]{0,2,1:T(8,128)(2,1)S(1)}) conditional(s32[]{:T(128)} %convert_element_type.376, () %tuple.230, (bf16[3,1024,3,192]{1,3,2,0:T(8,128)(2,1)}, s32[]{:T(128)}, f32[3,3,1024]{2,1,0:T(4,128)}, bf16[4,256,192]{1,2,0:T(8,128)(2,1)S(1)}) %tuple.278), branch_computations={%region_28.28_spmd, %region_29.31_spmd} | conditional | flops 1544844800 | bytes 92180552 | solution.py:37
  717.4 15.7 %conditional.20 = (f32[768,2304]{1,0:T(8,128)}, bf16[256,768]{1,0:T(8,128)(2,1)}, bf16[1,256,768]{2,1,0:T(8,128)(2,1)S(1)}, f32[1,768]{1,0:T(1,128)S(1)}, f32[1,...) conditional(s32[]{:T(128)} %convert_element_type.376, () %tuple.229, ...), branch_computations={%region_32.32_spmd, %region_33.41_spmd} | conditional | flops 1819015424 | bytes 26811976 | solution.py:37
  750.9 13.1 conditional.18
  768.5 13.0 select_add_fusion.14
  788.6 11.3 select_add_fusion.15
  812.1 46.5 %collective-permute-start.1 = (bf16[256,768]{1,0:T(8,128)(2,1)}, bf16[256,768]{1,0:T(8,128)(2,1)S(1)}, u32[]{:S(2)}, u32[]{:S(2)}) collective-permute-start(bf16[256,768]{1,0:T(8,128)(2,1)} %get-tuple-element.1837), channel_id=1, source_target_pairs={{64,0},{65,1},{66,2},{67,3},{68,4},{69,5},{70,6},{71,7},{72,8},{73... | collective-permute-start | bytes 1179656 | tf_op jit(solution)/shard_map/while/body/eval_jaxpr/ppermute | solution.py:19
  893.8 49.6 %reduce-scatter.12.cloned.1.call-done = bf16[1,48,768]{2,1,0:T(8,128)(2,1)} async-done(((bf16[1,768,768]{2,1,0:T(8,128)(2,1)}), bf16[1,48,768]{2,1,0:T(8,128)(2,1)}) %reduce-scatter.12.cloned.1.call-update) | async-done | bytes 73744 | tf_op jit(solution)/shard_map/reduce_scatter | solution.py:295
  943.5 78.8 %reduce-scatter.10.cloned.1.call-done = bf16[1,48,2304]{2,1,0:T(8,128)(2,1)} async-done(((bf16[1,768,2304]{2,1,0:T(8,128)(2,1)}), bf16[1,48,2304]{2,1,0:T(8,128)(2,1)}) %reduce-scatter.10.cloned.1.call-update) | async-done | bytes 221200 | tf_op jit(solution)/shard_map/reduce_scatter | solution.py:292
  1022.3 81.2 %reduce-scatter.14.cloned.1.call-done = bf16[1,48,3072]{2,1,0:T(8,128)(2,1)} async-done(((bf16[1,768,3072]{2,1,0:T(8,128)(2,1)}), bf16[1,48,3072]{2,1,0:T(8,128)(2,1)}) %reduce-scatter.14.cloned.1.call-update) | async-done | bytes 294928 | tf_op jit(solution)/shard_map/reduce_scatter | solution.py:298
  1103.5 81.2 %reduce-scatter.16.cloned.1.call-done = bf16[1,192,768]{2,1,0:T(8,128)(2,1)} async-done(((bf16[1,3072,768]{2,1,0:T(8,128)(2,1)}), bf16[1,192,768]{2,1,0:T(8,128)(2,1)}) %reduce-scatter.16.cloned.1.call-update) | async-done | bytes 294928 | tf_op jit(solution)/shard_map/reduce_scatter | solution.py:301
  1185.3 58.0 %all-reduce.7 = (bf16[1,2,768]{2,1,0:T(2,128)(2,1)S(1)}, bf16[1,6,768]{2,0,1:T(2,128)(2,1)S(1)}) all-reduce(bf16[1,2,768]{2,1,0:T(2,128)(2,1)S(1)} %convert_bitcast_fusion.5, bf16[1,6,768]{2,0,1:T(2,128)(2,1)S(1)} %convert_element_type.255), channel_id=6, replica_groups=mesh['section'=2,'seq'=4,'dp'=16] {'dp'}, use_global_device_ids=true, to_apply=%region_51.52.clone | all-reduce | flops 6144 | bytes 24576
  1245.3 14.6 %reduce-scatter.18.cloned.1.call-done = bf16[192,1]{1,0:T(8,128)(2,1)} async-done(((bf16[3072,1]{1,0:T(8,128)(2,1)}), bf16[192,1]{1,0:T(8,128)(2,1)}) %reduce-scatter.18.cloned.1.call-update) | async-done | bytes 400
  1271.2 36.0 %all-reduce.12.cloned.1.call-done = (bf16[1,48,2304]{2,1,0:T(8,128)(2,1)}, bf16[1,48,768]{2,1,0:T(8,128)(2,1)}, bf16[1,48,3072]{2,1,0:T(8,128)(2,1)}, bf16[1,192,768]{2,1,0:T(8,128)(2,1)}) async-done(((bf16[1,48,2304]{2,1,0:T(8,128)(2,1)}, bf16[1,48,768]{2,1,0:T(8,128)(2,1)}, bf16[1,48,3072]{2,1,0:T(8,128)(2,1)}, bf16[1,192,768]{2,1,0:T(8,128)(2,1)}), (bf16[1,48,2304]{2,1,0:T(8,128)(2,1)}, ...) | async-done | bytes 884752 | tf_op jit(solution)/shard_map/psum | solution.py:314
  (530 shorter events, 552.0 us)
Async XLA Ops:
  7.2 89.0 %all-gather.7.cloned.1.call-start = ((), (), s32[]{:S(2)}) async-start(), calls=%async_computation.10 | async-start | bytes 1253376 | tf_op jit(solution)/shard_map/all_gather | solution.py:45
  7.9 99.7 %all-gather.5.cloned.1.call-start = ((), (), s32[]{:S(2)}) async-start(), calls=%async_computation.9 | async-start | bytes 3760128 | tf_op jit(solution)/shard_map/all_gather | solution.py:44
  8.7 154.6 %all-gather.9.cloned.1.call-start = ((), (), s32[]{:S(2)}) async-start(), calls=%async_computation.11 | async-start | bytes 5013504 | tf_op jit(solution)/shard_map/all_gather | solution.py:46
  9.4 209.5 %all-gather.11.cloned.1.call-start = ((), (), s32[]{:S(2)}) async-start(), calls=%async_computation.12 | async-start | bytes 5013504 | tf_op jit(solution)/shard_map/all_gather | solution.py:47
  10.0 933.5 %reduce-scatter.12.cloned.1.call-start = ((), (), s32[]{:S(2)}) async-start(), calls=%async_computation.14 | async-start | bytes 1253376 | tf_op jit(solution)/shard_map/reduce_scatter | solution.py:295
  233.6 18.6 %all-to-all-start = ((bf16[256,3,768]{0,1,2:T(4,128)(2,1)}), bf16[256,3,768]{0,1,2:T(4,128)(2,1)S(1)}, u32[]{:S(2)}, u32[]{:S(2)}) async-start(bf16[256,3,768]{0,1,2:T(4,128)(2,1)} %copy.126), calls=%async_computation | async-start | bytes 3145728 | tf_op jit(solution)/shard_map/while/body/eval_jaxpr/all_to_all | solution.py:124
  254.2 9.7 all-to-all-start.1
  267.3 34.9 %collective-permute-start = (bf16[256,768]{1,0:T(8,128)(2,1)}, bf16[256,768]{1,0:T(8,128)(2,1)}, u32[]{:S(2)}, u32[]{:S(2)}) collective-permute-start(bf16[256,768]{1,0:T(8,128)(2,1)} %get-tuple-element.1796), channel_id=1, source_target_pairs={{0,64},{1,65},{2,66},{3,67},{4,68},{5,69},{6,70},{7,71},{8,72},{9,... | collective-permute-start | bytes 1179656 | tf_op jit(solution)/shard_map/while/body/eval_jaxpr/ppermute | solution.py:19
  315.4 17.0 %all-to-all-start = ((bf16[256,3,768]{0,1,2:T(4,128)(2,1)}), bf16[256,3,768]{0,1,2:T(4,128)(2,1)S(1)}, u32[]{:S(2)}, u32[]{:S(2)}) async-start(bf16[256,3,768]{0,1,2:T(4,128)(2,1)} %copy.126), calls=%async_computation | async-start | bytes 3145728 | tf_op jit(solution)/shard_map/while/body/eval_jaxpr/all_to_all | solution.py:124
  343.5 9.7 all-to-all-start.1
  371.2 12.2 collective-permute-start
  396.5 22.4 %all-to-all-start = ((bf16[256,3,768]{0,1,2:T(4,128)(2,1)}), bf16[256,3,768]{0,1,2:T(4,128)(2,1)S(1)}, u32[]{:S(2)}, u32[]{:S(2)}) async-start(bf16[256,3,768]{0,1,2:T(4,128)(2,1)} %copy.126), calls=%async_computation | async-start | bytes 3145728 | tf_op jit(solution)/shard_map/while/body/eval_jaxpr/all_to_all | solution.py:124
  430.0 9.7 all-to-all-start.1
  457.7 9.2 collective-permute-start
  525.3 13.8 %all-to-all-start.2 = ((bf16[256,4,192]{0,2,1:T(8,128)(2,1)}), bf16[256,4,192]{0,2,1:T(8,128)(2,1)S(1)}, u32[]{:S(2)}, u32[]{:S(2)}) async-start(bf16[256,4,192]{0,2,1:T(8,128)(2,1)} %bitcast.262), calls=%async_computation.2 | async-start | bytes 786432 | tf_op jit(solution)/shard_map/while/body/eval_jaxpr/all_to_all | solution.py:250
  562.8 19.9 %all-to-all-start.3 = ((bf16[1024,3,192]{2,1,0:T(4,128)(2,1)}), bf16[1024,3,192]{2,1,0:T(4,128)(2,1)}, u32[]{:S(2)}, u32[]{:S(2)}) async-start(bf16[1024,3,192]{2,1,0:T(4,128)(2,1)} %copy.132), calls=%async_computation.3 | async-start | bytes 4194304 | tf_op jit(solution)/shard_map/while/body/eval_jaxpr/all_to_all | solution.py:252
  602.3 10.3 collective-permute-start.1
  649.1 16.5 %all-to-all-start.2 = ((bf16[256,4,192]{0,2,1:T(8,128)(2,1)}), bf16[256,4,192]{0,2,1:T(8,128)(2,1)S(1)}, u32[]{:S(2)}, u32[]{:S(2)}) async-start(bf16[256,4,192]{0,2,1:T(8,128)(2,1)} %bitcast.262), calls=%async_computation.2 | async-start | bytes 786432 | tf_op jit(solution)/shard_map/while/body/eval_jaxpr/all_to_all | solution.py:250
  689.3 24.2 %all-to-all-start.3 = ((bf16[1024,3,192]{2,1,0:T(4,128)(2,1)}), bf16[1024,3,192]{2,1,0:T(4,128)(2,1)}, u32[]{:S(2)}, u32[]{:S(2)}) async-start(bf16[1024,3,192]{2,1,0:T(4,128)(2,1)} %copy.132), calls=%async_computation.3 | async-start | bytes 4194304 | tf_op jit(solution)/shard_map/while/body/eval_jaxpr/all_to_all | solution.py:252
  733.1 12.3 collective-permute-start.1
  765.0 16.5 %all-to-all-start.2 = ((bf16[256,4,192]{0,2,1:T(8,128)(2,1)}), bf16[256,4,192]{0,2,1:T(8,128)(2,1)S(1)}, u32[]{:S(2)}, u32[]{:S(2)}) async-start(bf16[256,4,192]{0,2,1:T(8,128)(2,1)} %bitcast.262), calls=%async_computation.2 | async-start | bytes 786432 | tf_op jit(solution)/shard_map/while/body/eval_jaxpr/all_to_all | solution.py:250
  784.2 19.9 %all-to-all-start.3 = ((bf16[1024,3,192]{2,1,0:T(4,128)(2,1)}), bf16[1024,3,192]{2,1,0:T(4,128)(2,1)}, u32[]{:S(2)}, u32[]{:S(2)}) async-start(bf16[1024,3,192]{2,1,0:T(4,128)(2,1)} %copy.132), calls=%async_computation.3 | async-start | bytes 4194304 | tf_op jit(solution)/shard_map/while/body/eval_jaxpr/all_to_all | solution.py:252
  812.1 57.6 %collective-permute-start.1 = (bf16[256,768]{1,0:T(8,128)(2,1)}, bf16[256,768]{1,0:T(8,128)(2,1)S(1)}, u32[]{:S(2)}, u32[]{:S(2)}) collective-permute-start(bf16[256,768]{1,0:T(8,128)(2,1)} %get-tuple-element.1837), channel_id=1, source_target_pairs={{64,0},{65,1},{66,2},{67,3},{68,4},{69,5},{70,6},{71,7},{72,8},{73... | collective-permute-start | bytes 1179656 | tf_op jit(solution)/shard_map/while/body/eval_jaxpr/ppermute | solution.py:19
  873.4 148.9 %reduce-scatter.10.cloned.1.call-start = ((), (), s32[]{:S(2)}) async-start(), calls=%async_computation.13 | async-start | bytes 3760128 | tf_op jit(solution)/shard_map/reduce_scatter | solution.py:292
  878.6 224.8 %reduce-scatter.14.cloned.1.call-start = ((), (), s32[]{:S(2)}) async-start(), calls=%async_computation.15 | async-start | bytes 5013504 | tf_op jit(solution)/shard_map/reduce_scatter | solution.py:298
  885.3 299.3 %reduce-scatter.16.cloned.1.call-start = ((), (), s32[]{:S(2)}) async-start(), calls=%async_computation.16 | async-start | bytes 5013504 | tf_op jit(solution)/shard_map/reduce_scatter | solution.py:301
  891.7 293.6 %copy-start.10 = (f32[6,768]{1,0:T(8,128)S(1)}, f32[6,768]{1,0:T(8,128)}, u32[]{:S(2)}) copy-start(f32[6,768]{1,0:T(8,128)} %get-tuple-element.914) | copy-start | bytes 55300
  891.7 293.6 %copy-start.18 = (f32[2,768]{1,0:T(2,128)S(1)}, f32[2,768]{1,0:T(2,128)}, u32[]{:S(2)}) copy-start(f32[2,768]{1,0:T(2,128)} %get-tuple-element.913) | copy-start | bytes 18436
  891.7 351.7 %copy-start.6 = (bf16[3,256,768]{2,1,0:T(8,128)(2,1)S(1)}, bf16[3,256,768]{2,1,0:T(8,128)(2,1)}, u32[]{:S(2)}) copy-start(bf16[3,256,768]{2,1,0:T(8,128)(2,1)} %get-tuple-element.898) | copy-start | bytes 3538948
  891.7 352.6 %copy-start.7 = (bf16[3,256,768]{2,1,0:T(8,128)(2,1)S(1)}, bf16[3,256,768]{2,1,0:T(8,128)(2,1)}, u32[]{:S(2)}) copy-start(bf16[3,256,768]{2,1,0:T(8,128)(2,1)} %get-tuple-element.908) | copy-start | bytes 3538948
  891.7 368.1 %reduce-scatter.18.cloned.1.call-start = ((), (), s32[]{:S(2)}) async-start(), calls=%async_computation.17 | async-start | bytes 835584
  893.8 413.4 %all-reduce.12.cloned.1.call-start = ((), (), s32[]{:S(2)}) async-start(), calls=%async_computation.18 | async-start | bytes 1769472 | tf_op jit(solution)/shard_map/psum | solution.py:314
  (47 other events, 416.9 us)
Sparse Core Ops, SparseCore 0:
  10.2 45.3 all-gather.6
  57.7 49.8 all-gather.4
  109.8 53.5 all-gather.8
  165.3 53.5 all-gather.10
  873.5 69.9 reduce-scatter.11
  946.7 75.5 reduce-scatter.9
  1025.6 77.8 reduce-scatter.13
  1106.8 77.7 reduce-scatter.15
  1187.8 71.9 reduce-scatter.17
  1262.3 44.8 all-reduce.11
where the time goes:
time: 1330 us; the launch traced here: 1320 us
  waiting for transfers between devices  560 us (42%)
  other arithmetic  183 us (14%)
  local copies, waits for them, and re-layouts  156 us (12%)
  blocking collectives  137 us (10%)
  matrix products  130 us (10%)
  starting transfers between devices  98.8 us (7%)
  loops' own time  40.7 us (3%)
  between operations  16 us (1%)
    add x21, other arithmetic, backward_tick(): sums = tuple((total + term for total, term in zip(sums, terms)))  105 us
    unnamed x2, blocking collectives  92.8 us
    reduce_scatter x1, waiting for transfers between devices, body(): lax.psum_scatter(lifted[2].astype(jnp.bfloat16), 'dp', scatter_dimension=...  81.2 us
    reduce_scatter x1, waiting for transfers between devices, body(): lax.psum_scatter(lifted[3].astype(jnp.bfloat16), 'dp', scatter_dimension=...  81.2 us
    reduce_scatter x1, waiting for transfers between devices, body(): lax.psum_scatter(lifted[0].astype(jnp.bfloat16), 'dp', scatter_dimension=...  78.8 us
    all_gather x1, waiting for transfers between devices, body(): lax.all_gather(w_fc, 'dp', axis=1, tiled=True)  55.7 us
    all_gather x1, waiting for transfers between devices, body(): lax.all_gather(w_proj, 'dp', axis=1, tiled=True)  55.6 us
    ppermute x6, starting transfers between devices, passed_along(): return lax.ppermute(block, axis, route)  53 us
  transfers between devices with their start and end apart: 28, of which 19 were waited for; matrix products, arithmetic and copies ran while one was open for 14% of the time, Pallas kernels for 0%

commit v1 on v0

v1 whole, which is shorter than its diff:
```python
import functools
import math

import jax
import jax.numpy as jnp
from jax import lax
from jax.experimental import pallas as pl
from jax.experimental.pallas import tpu as pltpu
from jax.sharding import PartitionSpec as P

MESH = pl.DeviceIdType.MESH
BF = jnp.bfloat16
F32 = jnp.float32
D = 768
T = 512
L = 1024
HALF = 384
ROWS = 608
HROWS = ROWS // 2
EPS = 1e-05
SCALE = 0.125
C2 = SCALE * math.log2(math.e)
VLIM = 60 * 1024 * 1024
ANY = pl.BlockSpec(memory_space=pl.ANY)
VM = pl.BlockSpec(memory_space=pltpu.VMEM)


def where_am_i():
    core = lax.axis_index("section")
    z = lax.axis_index("seq")
    dp = lax.axis_index("dp")
    return core, z, dp // 4, dp % 4


def greet(peers):
    barrier = pltpu.get_barrier_semaphore()
    for peer in peers:
        pl.semaphore_signal(barrier, inc=1, device_id=peer, device_id_type=MESH)
    pl.semaphore_wait(barrier, len(peers))


def remote(src, dst, send, recv, peer):
    return pltpu.make_async_remote_copy(
        src_ref=src, dst_ref=dst, send_sem=send, recv_sem=recv, device_id=peer, device_id_type=MESH
    )


def comm_params(ident):
    return pltpu.CompilerParams(
        collective_id=ident, has_side_effects=True, vmem_limit_bytes=VLIM
    )


def gather_kernel(shard, ins, cots, full, stream, lsem, ssem, rsem, xs, xr):
    core, z, y, x = where_am_i()
    block = z % 2
    sib = 1 - core
    dp = y * 4 + x
    sibling = (sib, z, dp)
    first = core == 0

    def along(axis, step):
        if axis == 0:
            return (core, z, y * 4 + (x + step) % 4)
        return (core, z, ((y + step) % 4) * 4 + x)

    peers = [sibling]
    for step in (1, 2, 3):
        peers += [along(0, step), along(1, step), (core, (z + step) % 4, dp)]
    greet(peers)

    mine = pl.ds(pl.multiple_of(core * HROWS, 16), HROWS)
    other = pl.ds(pl.multiple_of(sib * HROWS, 16), HROWS)

    own_local = pltpu.make_async_copy(shard.at[mine], full.at[y, x, mine], lsem.at[0])
    give = remote(
        shard.at[other], full.at[y, x, other], ssem.at[0], rsem.at[0], sibling
    )
    take = remote(
        shard.at[mine], full.at[y, x, mine], ssem.at[0], rsem.at[0], sibling
    )

    @pl.when(core == block)
    def _():
        own_local.start()
        give.start()
        own_local.wait()

    @pl.when(core != block)
    def _():
        take.wait_recv()

    def shard_at(axis, step):
        if axis == 0:
            return full.at[y, (x + step) % 4, mine]
        return full.at[(y + step) % 4, x, mine]

    def line_at(axis, step, part):
        if axis == 0:
            return full.at[pl.ds(2 * part, 2), (x + step) % 4, mine]
        return full.at[(y + step) % 4, pl.ds(2 * part, 2), mine]

    def relay(view, slot):
        return remote(view, view, ssem.at[slot], rsem.at[slot], sibling)

    def rest(axis):
        cross = 1 - axis
        hops = [
            remote(shard_at(axis, 0), shard_at(axis, 0), ssem.at[k], rsem.at[k], along(axis, k))
            for k in (1, 2, 3)
        ]
        for hop in hops:
            hop.start()
        own_relay = relay(shard_at(axis, 0), 14)
        own_relay.start()
        relays = [own_relay]

        for k in (1, 3, 2):
            land = shard_at(axis, 4 - k)
            remote(land, land, ssem.at[k], rsem.at[k], sibling).wait_recv()
        sends = []
        for part in (0, 1):
            for slot, step in ((4, 1), (6, 3)):
                view = line_at(cross, 0, part)
                hop = remote(
                    view, view, ssem.at[slot + part], rsem.at[slot + part], along(cross, step)
                )
                hop.start()
                sends.append(hop)
        for k in (1, 3, 2):
            copy = relay(shard_at(axis, 4 - k), 15 + k - 1)
            copy.start()
            relays.append(copy)
        for part, slot, came, to in ((0, 4, 3, 1), (1, 6, 1, 3), (1, 4, 3, None), (0, 6, 1, None)):
            land = line_at(cross, came, part)
            remote(land, land, ssem.at[slot + part], rsem.at[slot + part], sibling).wait_recv()
            if to is not None:
                hop = remote(land, land, ssem.at[8 + part], rsem.at[8 + part], along(cross, to))
                hop.start()
                sends.append(hop)
            copy = relay(land, 18 + slot - 4 + part)
            copy.start()
            relays.append(copy)
        for part in (0, 1):
            land = line_at(cross, 2, part)
            remote(land, land, ssem.at[8 + part], rsem.at[8 + part], sibling).wait_recv()
            copy = relay(land, 22 + part)
            copy.start()
            relays.append(copy)
        for hop in hops + sends + relays:
            hop.wait_send()

    def arrivals(axis):
        cross = 1 - axis

        def there(view_axis, step):
            if view_axis == 0:
                return full.at[y, (x + step) % 4, other]
            return full.at[(y + step) % 4, x, other]

        def lines(view_axis, step, part):
            if view_axis == 0:
                return full.at[pl.ds(2 * part, 2), (x + step) % 4, other]
            return full.at[(y + step) % 4, pl.ds(2 * part, 2), other]

        def done(view, slot):
            remote(view, view, ssem.at[slot], rsem.at[slot], sibling).wait_recv()

        done(there(axis, 0), 14)
        for k in (1, 3, 2):
            done(there(axis, 4 - k), 15 + k - 1)
        for part, slot, came in ((0, 4, 3), (1, 6, 1), (1, 4, 3), (0, 6, 1)):
            done(lines(cross, came, part), 18 + slot - 4 + part)
        for part in (0, 1):
            done(lines(cross, 2, part), 22 + part)

    quarter = pl.ds(pl.multiple_of((z % 2) * 256, 256), 256)
    sends_tokens = (z // 2) == core
    for step in (1, 2, 3):
        to = (z + step) % 4
        for source, parity in ((ins, 0), (cots, 1)):

            @pl.when(sends_tokens & (to % 2 == parity))
            def _():
                remote(
                    source.at[to // 2],
                    stream.at[quarter],
                    xs.at[step],
                    xr.at[z % 2],
                    (core, to, dp),
                ).start()

    for source, parity in ((ins, 0), (cots, 1)):

        @pl.when(sends_tokens & (z % 2 == parity))
        def _():
            copy = pltpu.make_async_copy(source.at[z // 2], stream.at[quarter], lsem.at[1])
            copy.start()
            copy.wait()

    @pl.when(first)
    def _():
        rest(0)
        arrivals(1)

    @pl.when(jnp.logical_not(first))
    def _():
        rest(1)
        arrivals(0)

    @pl.when(core == block)
    def _():
        give.wait_send()

    for step in (1, 2, 3):

        @pl.when(sends_tokens)
        def _():
            remote(ins.at[0], stream.at[quarter], xs.at[step], xr.at[0], sibling).wait_send()

    for j in (0, 1):

        @pl.when(z != 2 * core + j)
        def _():
            land = stream.at[pl.ds(256 * j, 256)]
            remote(land, land, xs.at[0], xr.at[j], sibling).wait_recv()


def gather(shard, ins, cots):
    return pl.pallas_call(
        gather_kernel,
        name="gather_weights",
        out_shape=(
            jax.ShapeDtypeStruct((4, 4, ROWS, D), BF),
            jax.ShapeDtypeStruct((T, D), BF),
        ),
        in_specs=[ANY] * 3,
        out_specs=(ANY, ANY),
        scratch_shapes=[
            pltpu.SemaphoreType.DMA((2,)),
            pltpu.SemaphoreType.DMA((24,)),
            pltpu.SemaphoreType.DMA((24,)),
            pltpu.SemaphoreType.DMA((4,)),
            pltpu.SemaphoreType.DMA((2,)),
        ],
        compiler_params=comm_params(0),
    )(shard, ins, cots)


def cross_kernel(src, dst, lsem, ssem, rsem):
    core, z, y, x = where_am_i()
    sibling = (1 - core, z, y * 4 + x)
    greet([sibling])
    local = pltpu.make_async_copy(src.at[core], dst.at[core], lsem)
    local.start()
    out = remote(src.at[1 - core], dst.at[core], ssem, rsem, sibling)
    out.start()
    local.wait()
    out.wait_send()
    remote(src.at[1 - core], dst.at[1 - core], ssem, rsem, sibling).wait_recv()


def cross(pieces, ident):
    return pl.pallas_call(
        cross_kernel,
        name="cross_cores",
        out_shape=jax.ShapeDtypeStruct(pieces.shape, pieces.dtype),
        in_specs=[ANY],
        out_specs=ANY,
        scratch_shapes=[pltpu.SemaphoreType.DMA] * 3,
        compiler_params=comm_params(ident),
    )(pieces)


def hand_kernel(giver, made, held, dst, lsem, ssem, rsem):
    core, z, y, x = where_am_i()
    partner = (core, z + 1 - 2 * (z % 2), y * 4 + x)
    greet([partner])
    out = remote(made, dst, ssem, rsem, partner)

    @pl.when(z % 2 == giver)
    def _():
        out.start()
        local = pltpu.make_async_copy(held, dst, lsem)
        local.start()
        local.wait()
        out.wait_send()

    @pl.when(z % 2 != giver)
    def _():
        out.wait_recv()


def hand_over(made, held, giver):
    return pl.pallas_call(
        functools.partial(hand_kernel, giver),
        name="hand_over",
        out_shape=jax.ShapeDtypeStruct(made.shape, made.dtype),
        in_specs=[ANY, ANY],
        out_specs=ANY,
        scratch_shapes=[pltpu.SemaphoreType.DMA] * 3,
        compiler_params=comm_params(3 + giver),
    )(made, held)


def dot(a, b):
    return jnp.dot(a, b, preferred_element_type=F32)


def dot_nt(a, b):
    return lax.dot_general(a, b, (((1,), (1,)), ((), ())), preferred_element_type=F32)


def dot_tn(a, b):
    return lax.dot_general(a, b, (((0,), (0,)), ((), ())), preferred_element_type=F32)


def normalized(v):
    centre = v - jnp.mean(v, axis=-1, keepdims=True)
    inv = lax.rsqrt(jnp.mean(centre * centre, axis=-1, keepdims=True) + EPS)
    return centre * inv, inv


def norm_back(grad, gain, unit, inv):
    g = grad * gain
    return inv * (
        g
        - jnp.mean(g, axis=-1, keepdims=True)
        - unit * jnp.mean(g * unit, axis=-1, keepdims=True)
    )


def matrix(ref, m):
    return ref[:, m * 48 : (m + 1) * 48, :].reshape(D, D)


def down_matrix(ref, m):
    return ref[4 * m : 4 * m + 4].reshape(D, D)


def weight_spec(rows, index):
    return pl.BlockSpec(
        (16, rows, D), lambda i: (0, index, 0), pipeline_mode=pl.Buffered(1)
    )


def whole(shape):
    return pl.BlockSpec(shape, lambda i: (0,) * len(shape))


TILE = 256
STEPS = T // TILE


def tile(width):
    return pl.BlockSpec((TILE, width), lambda i: (i, 0))


def pair_tile(width):
    return pl.BlockSpec((2, TILE, width), lambda i: (0, i, 0))


def local_params():
    return pltpu.CompilerParams(vmem_limit_bytes=VLIM)


def front_kernel(x, w, par, packed, normed_out):
    unit, _ = normalized(x[...].astype(F32))
    normed = (unit * par[0:1] + par[2:3]).astype(BF)
    normed_out[...] = normed
    a = (dot(normed, matrix(w, 0)) + par[12:13]).astype(BF)
    packed[0, :, :D] = a
    b = (dot(normed, matrix(w, 1)) + par[13:14]).astype(BF)
    packed[0, :, D:] = b[:, :HALF]
    packed[1, :, :HALF] = b[:, HALF:]
    c = (dot(normed, matrix(w, 2)) + par[14:15]).astype(BF)
    packed[1, :, HALF:] = c


def front(x, w, par):
    return pl.pallas_call(
        front_kernel,
        name="front",
        grid=(STEPS,),
        out_shape=(
            jax.ShapeDtypeStruct((2, T, 3 * HALF), BF),
            jax.ShapeDtypeStruct((T, D), BF),
        ),
        in_specs=[tile(D), weight_spec(144, 0), whole((16, D))],
        out_specs=(pair_tile(3 * HALF), tile(D)),
        compiler_params=local_params(),
    )(x, w, par)


QB = 256


def head_masks(ref_value):
    lane = lax.broadcasted_iota(jnp.int32, ref_value.shape, 1)
    zero = jnp.zeros_like(ref_value)
    return (
        jnp.where(lane < 64, ref_value, zero),
        jnp.where(lane >= 64, ref_value, zero),
    )


def causal(rows, cols, offset):
    row = lax.broadcasted_iota(jnp.int32, (rows, cols), 0) + offset
    return lax.broadcasted_iota(jnp.int32, (rows, cols), 1) <= row


def attend_kernel(q_ref, k_ref, v_ref, mixed, logs):
    for i in range(L // QB):
        at = slice(i * QB, (i + 1) * QB)
        stop = (i + 1) * QB
        keys = k_ref[:stop]
        queries = head_masks(q_ref[at])
        values = head_masks(v_ref[:stop])
        keep = causal(QB, stop, i * QB)
        total = None
        saved = []
        for h in range(2):
            s = jnp.where(keep, dot_nt(queries[h], keys), -1e30)
            peak = jnp.max(s, axis=-1, keepdims=True)
            p = jnp.exp2((s - peak) * C2)
            norm = jnp.sum(p, axis=-1, keepdims=True)
            o = dot(p.astype(BF), values[h]) * (1.0 / norm)
            total = o if total is None else total + o
            saved.append(peak * C2 + jnp.log2(norm))
        mixed[at] = total.astype(BF)
        lane = lax.broadcasted_iota(jnp.int32, (QB, 128), 1)
        logs[0, at] = jnp.where(lane < 64, saved[0], saved[1])


def attend(heads):
    def col(k):
        return pl.BlockSpec((L, 128), lambda p: (0, p + 3 * k))

    return pl.pallas_call(
        attend_kernel,
        name="attend",
        grid=(3,),
        out_shape=(
            jax.ShapeDtypeStruct((L, HALF), BF),
            jax.ShapeDtypeStruct((3, L, 128), F32),
        ),
        in_specs=[col(0), col(1), col(2)],
        out_specs=(col(0), pl.BlockSpec((1, L, 128), lambda p: (p, 0, 0))),
        compiler_params=local_params(),
    )(heads, heads, heads)


def attend_back_kernel(q_ref, k_ref, v_ref, o_ref, do_ref, logs, out, dk, dv):
    p_at = pl.program_id(0)
    dk[...] = jnp.zeros_like(dk)
    dv[...] = jnp.zeros_like(dv)

    def columns(part):
        return pl.ds(pl.multiple_of(part * HALF + p_at * 128, 128), 128)

    for i in range(L // QB):
        at = slice(i * QB, (i + 1) * QB)
        stop = (i + 1) * QB
        keys = k_ref[:stop]
        values = v_ref[:stop]
        keys_of = head_masks(keys)
        queries = head_masks(q_ref[at])
        tops = head_masks(do_ref[at])
        keep = causal(QB, stop, i * QB)
        inner = head_masks(do_ref[at].astype(F32) * o_ref[at].astype(F32))
        dq = None
        for h in range(2):
            s = dot_nt(queries[h], keys)
            total = logs[0, at, 64 * h : 64 * h + 1]
            p = jnp.where(keep, jnp.exp2(s * C2 - total), 0.0)
            gw = dot_nt(tops[h], values)
            delta = jnp.sum(inner[h], axis=-1, keepdims=True)
            ds = (p * (gw - delta)).astype(BF)
            part = dot(ds, keys_of[h])
            dq = part if dq is None else dq + part
            dk[:stop] += dot_tn(ds, queries[h])
            dv[:stop] += dot_tn(p.astype(BF), tops[h])
        out[at, columns(0)] = (dq * SCALE).astype(BF)
    out[:, columns(1)] = (dk[...] * SCALE).astype(BF)
    out[:, columns(2)] = dv[...].astype(BF)


def attend_back(heads, mixed, grad_mixed, logs):
    def col(k):
        return pl.BlockSpec((L, 128), lambda p: (0, p + 3 * k))

    return pl.pallas_call(
        attend_back_kernel,
        name="attend_back",
        grid=(3,),
        out_shape=jax.ShapeDtypeStruct((L, 3 * HALF), BF),
        in_specs=[
            col(0),
            col(1),
            col(2),
            col(0),
            col(0),
            pl.BlockSpec((1, L, 128), lambda p: (p, 0, 0)),
        ],
        out_specs=pl.BlockSpec((L, 3 * HALF), lambda p: (0, 0)),
        scratch_shapes=[pltpu.VMEM((L, 128), F32)] * 2,
        compiler_params=local_params(),
    )(heads, heads, heads, mixed, grad_mixed, logs)


def gelu(v):
    return 0.5 * v * (1.0 + jnp.tanh(0.79788456 * (v + 0.044715 * v * v * v)))


def gelu_slope(v):
    square = v * v
    t = jnp.tanh(0.79788456 * v * (1.0 + 0.044715 * square))
    return 0.5 * (1.0 + t) + 0.5 * v * (1.0 - t * t) * 0.79788456 * (
        1.0 + 3 * 0.044715 * square
    )


def rear_kernel(x, mixed, wo, wf, wp, par, result, *kept):
    mix = jnp.concatenate([mixed[0], mixed[1]], axis=1)
    middle = x[...].astype(F32) + (dot(mix, matrix(wo, 0)) + par[5:6])
    unit, _ = normalized(middle)
    normed = (unit * par[1:2] + par[6:7]).astype(BF)
    total = middle + par[7:8]
    for m in range(4):
        pre = dot(normed, matrix(wf, m)) + par[8 + m : 9 + m]
        active = gelu(pre).astype(BF)
        if kept:
            kept[2][:, m * D : (m + 1) * D] = pre.astype(BF)
            kept[3][:, m * D : (m + 1) * D] = active
        total = total + dot(active, down_matrix(wp, m))
    result[...] = total.astype(BF)
    if kept:
        kept[0][...] = middle
        kept[1][...] = normed


def rear(x, mixed, w, par, keep):
    outs = [((T, D), BF)]
    specs = [tile(D)]
    if keep:
        outs += [((T, D), F32), ((T, D), BF), ((T, 4 * D), BF), ((T, 4 * D), BF)]
        specs += [tile(D), tile(D), tile(4 * D), tile(4 * D)]
    return pl.pallas_call(
        rear_kernel,
        name="rear",
        grid=(STEPS,),
        out_shape=tuple(jax.ShapeDtypeStruct(s, t) for s, t in outs),
        in_specs=[
            tile(D),
            pair_tile(HALF),
            weight_spec(48, 3),
            weight_spec(192, 1),
            weight_spec(192, 2),
            whole((16, D)),
        ],
        out_specs=tuple(specs),
        compiler_params=local_params(),
    )(x, mixed, w, w, w, par)


def column_sum(v):
    return jnp.sum(v, axis=0, keepdims=True)


def rear_back_kernel(e, middle, pre, wo, wf, wp, par, gmixed, gmiddle, mlow, gpre, sums):
    @pl.when(pl.program_id(0) == 0)
    def _():
        sums[...] = jnp.zeros_like(sums)

    top = e[...]
    top_wide = top.astype(F32)
    gnorm = None
    for m in range(4):
        cols = slice(m * D, (m + 1) * D)
        gact = dot_nt(top, down_matrix(wp, m))
        low = (gact * gelu_slope(pre[:, cols].astype(F32))).astype(BF)
        gpre[:, cols] = low
        sums[4 + m : 5 + m] += column_sum(low.astype(F32))
        part = dot_nt(low, matrix(wf, m))
        gnorm = part if gnorm is None else gnorm + part
    unit, inv = normalized(middle[...])
    sums[0:1] += column_sum(top_wide)
    sums[1:2] += column_sum(gnorm * unit)
    sums[2:3] += column_sum(gnorm)
    gmid = top_wide + norm_back(gnorm, par[1:2], unit, inv)
    sums[3:4] += column_sum(gmid)
    gmiddle[...] = gmid
    low = gmid.astype(BF)
    mlow[...] = low
    gm = dot_nt(low, matrix(wo, 0)).astype(BF)
    gmixed[0] = gm[:, :HALF]
    gmixed[1] = gm[:, HALF:]


def rear_back(e, middle, pre, w, par):
    return pl.pallas_call(
        rear_back_kernel,
        name="rear_back",
        grid=(STEPS,),
        out_shape=(
            jax.ShapeDtypeStruct((2, T, HALF), BF),
            jax.ShapeDtypeStruct((T, D), F32),
            jax.ShapeDtypeStruct((T, D), BF),
            jax.ShapeDtypeStruct((T, 4 * D), BF),
            jax.ShapeDtypeStruct((8, D), F32),
        ),
        in_specs=[
            tile(D),
            tile(D),
            tile(4 * D),
            weight_spec(48, 3),
            weight_spec(192, 1),
            weight_spec(192, 2),
            whole((16, D)),
        ],
        out_specs=(pair_tile(HALF), tile(D), tile(D), tile(4 * D), whole((8, D))),
        compiler_params=local_params(),
    )(e, middle, pre, w, w, w, par)


def front_back_kernel(gp, gmiddle, x, w, par, grad, sums):
    @pl.when(pl.program_id(0) == 0)
    def _():
        sums[...] = jnp.zeros_like(sums)

    gnorm = None
    for m, piece in enumerate(packed_pieces(gp)):
        sums[2 + m : 3 + m] += column_sum(piece.astype(F32))
        part = dot_nt(piece, matrix(w, m))
        gnorm = part if gnorm is None else gnorm + part
    unit, inv = normalized(x[...].astype(F32))
    sums[0:1] += column_sum(gnorm * unit)
    sums[1:2] += column_sum(gnorm)
    grad[...] = (gmiddle[...] + norm_back(gnorm, par[0:1], unit, inv)).astype(BF)


def packed_pieces(gp):
    return (
        gp[0, :, :D],
        jnp.concatenate([gp[0, :, D:], gp[1, :, :HALF]], axis=1),
        gp[1, :, HALF:],
    )


def front_back(gp, gmiddle, x, w, par):
    return pl.pallas_call(
        front_back_kernel,
        name="front_back",
        grid=(STEPS,),
        out_shape=(
            jax.ShapeDtypeStruct((T, D), BF),
            jax.ShapeDtypeStruct((8, D), F32),
        ),
        in_specs=[
            pair_tile(3 * HALF),
            tile(D),
            tile(D),
            weight_spec(144, 0),
            whole((16, D)),
        ],
        out_specs=(tile(D), whole((8, D))),
        compiler_params=local_params(),
    )(gp, gmiddle, x, w, par)


def weight_grads_kernel(normed, gp, mixed, mlow, normed2, gpre, active, top, small, out):
    def put(m, value):
        out[:, m * 48 : (m + 1) * 48, :] = value.astype(BF).reshape(16, 48, D)

    for m, piece in enumerate(packed_pieces(gp)):
        put(m, dot_tn(normed[...], piece))
    put(3, dot_tn(jnp.concatenate([mixed[0], mixed[1]], axis=1), mlow[...]))
    for m in range(4):
        put(4 + m, dot_tn(normed2[...], gpre[:, m * D : (m + 1) * D]))
    for m in range(4):
        value = dot_tn(active[:, m * D : (m + 1) * D], top[...])
        out[4 * m : 4 * m + 4, 384:576, :] = value.astype(BF).reshape(4, 192, D)
    out[:, 576:608, :] = small[...]


def weight_grads(*operands):
    return pl.pallas_call(
        weight_grads_kernel,
        name="weight_grads",
        out_shape=jax.ShapeDtypeStruct((16, ROWS, D), BF),
        in_specs=[VM] * len(operands),
        out_specs=VM,
        compiler_params=local_params(),
    )(*operands)


def reduce_kernel(
    grads, result, ingrad, total, out_a, out_b,
    own, r0, r1, r2, s1, s2, r3, lsem, s0s, s0r, s1s, s1r, s2s, s2r, s3s, s3r, os, orr, ol,
):
    core, z, y, x = where_am_i()
    block = z % 2
    sib = 1 - core
    dp = y * 4 + x
    sibling = (sib, z, dp)
    first = core == 0
    line = jnp.where(first, y, x)
    place = jnp.where(first, x, y)

    def on_line(step):
        to = (line + step) % 4
        return (core, z, jnp.where(first, to * 4 + x, y * 4 + to))

    def on_place(step):
        to = (place + step) % 4
        return (core, z, jnp.where(first, y * 4 + to, to * 4 + x))

    peers = [sibling]
    for step in (1, 2, 3):
        peers += [on_line(step), on_place(step)]
        for k in (0, 1):
            peers.append((k, (z + step) % 4, dp))
    greet(peers)

    mine = pl.ds(pl.multiple_of(core * HROWS, 16), HROWS)
    other = pl.ds(pl.multiple_of(sib * HROWS, 16), HROWS)

    def zero_copies(step):
        at = (line + step) % 4
        return at

    @pl.when(first)
    def _():
        for k in range(4):
            remote(grads.at[:, k, other], r0.at[k], s0s.at[k], s0r.at[k], sibling).start()
        for k in range(4):
            pltpu.make_async_copy(grads.at[k, :, mine], own.at[k], lsem.at[k]).start()

    @pl.when(jnp.logical_not(first))
    def _():
        for k in range(4):
            remote(grads.at[k, :, other], r0.at[k], s0s.at[k], s0r.at[k], sibling).start()
        for k in range(4):
            pltpu.make_async_copy(grads.at[:, k, mine], own.at[k], lsem.at[k]).start()

    for j in (0, 1):
        for n, (src, dst) in enumerate(((result, out_a), (ingrad, out_b))):
            here = (core == block) & (z == 2 * core + j)
            view = src.at[pl.ds(256 * j, 256)]

            @pl.when(here)
            def _():
                pltpu.make_async_copy(view, dst.at[z // 2], ol.at[n]).start()

            @pl.when(jnp.logical_not(here))
            def _():
                remote(
                    view, dst.at[z // 2], os.at[2 * j + n], orr.at[z // 2, n],
                    (block, 2 * core + j, dp),
                ).start()

    for k in range(4):
        pltpu.make_async_copy(own.at[k], own.at[k], lsem.at[k]).wait()
        remote(r0.at[k], r0.at[k], s0s.at[k], s0r.at[k], sibling).wait()

        @pl.loop(0, 4)
        def _(i):
            own[k, i] = (own[k, i].astype(F32) + r0[k, i].astype(F32)).astype(BF)

    for step in (2, 1, 3):
        at = (line + step) % 4
        remote(
            own.at[at], r1.at[step - 1], s1s.at[step], s1r.at[step], on_line(step)
        ).start()
    for step in (1, 3, 2):
        remote(own.at[0], r1.at[step - 1], s1s.at[step], s1r.at[step], sibling).wait()

    @pl.loop(0, 4)
    def _(i):
        s1[i] = (
            (own[line, i].astype(F32) + r1[0, i].astype(F32))
            + (r1[1, i].astype(F32) + r1[2, i].astype(F32))
        ).astype(BF)

    for step in (2, 1, 3):
        at = (place + step) % 4
        remote(
            s1.at[at], r2.at[step - 1], s2s.at[step], s2r.at[step], on_place(step)
        ).start()
    for step in (1, 3, 2):
        remote(s1.at[0], r2.at[step - 1], s2s.at[step], s2r.at[step], sibling).wait()
    s2[...] = (
        (s1[place].astype(F32) + r2[0].astype(F32))
        + (r2[1].astype(F32) + r2[2].astype(F32))
    ).astype(BF)

    for step in (2, 1, 3, 0):
        to = (z + step) % 4
        if step == 0:

            @pl.when(core == block)
            def _():
                pltpu.make_async_copy(s2, r3.at[core, z // 2], ol.at[2]).start()

            @pl.when(core != block)
            def _():
                remote(
                    s2, r3.at[core, z // 2], s3s.at[step], s3r.at[core, z // 2], sibling
                ).start()

        else:
            remote(
                s2, r3.at[core, z // 2], s3s.at[step], s3r.at[core, z // 2], (block, to, dp)
            ).start()
    for step in (1, 2, 3):
        remote(s2, s2, s3s.at[step], s3r.at[0, 0], sibling).wait_send()

    @pl.when(core == block)
    def _():
        pltpu.make_async_copy(s2, r3.at[core, z // 2], ol.at[2]).wait()

    @pl.when(core != block)
    def _():
        remote(s2, s2, s3s.at[0], s3r.at[0, 0], sibling).wait_send()

    for c in (0, 1):
        for s in (0, 1):
            here = (core == block) & (core == c) & (z // 2 == s)

            @pl.when(jnp.logical_not(here))
            def _():
                remote(s2, r3.at[c, s], s3s.at[0], s3r.at[c, s], sibling).wait_recv()

    for c in (0, 1):
        total[c * HROWS : (c + 1) * HROWS] = r3[c, 0].astype(F32) + r3[c, 1].astype(F32)

    for j in (0, 1):
        for n, (src, dst) in enumerate(((result, out_a), (ingrad, out_b))):
            here = (core == block) & (z == 2 * core + j)
            view = src.at[pl.ds(256 * j, 256)]

            @pl.when(here)
            def _():
                pltpu.make_async_copy(view, dst.at[z // 2], ol.at[n]).wait()

            @pl.when(jnp.logical_not(here))
            def _():
                remote(
                    view, dst.at[z // 2], os.at[2 * j + n], orr.at[0, n], sibling
                ).wait_send()

    for s in (0, 1):
        for n, dst in enumerate((out_a, out_b)):
            here = (core == z // 2) & (z == 2 * s + core)

            @pl.when(jnp.logical_not(here))
            def _():
                remote(
                    dst.at[s], dst.at[s], os.at[0], orr.at[s, n], sibling
                ).wait_recv()


def reduce(grads, result, ingrad):
    dma = pltpu.SemaphoreType.DMA
    return pl.pallas_call(
        reduce_kernel,
        name="reduce_grads",
        out_shape=(
            jax.ShapeDtypeStruct((ROWS, D), F32),
            jax.ShapeDtypeStruct((2, 256, D), BF),
            jax.ShapeDtypeStruct((2, 256, D), BF),
        ),
        in_specs=[ANY] * 3,
        out_specs=(VM, ANY, ANY),
        scratch_shapes=[
            pltpu.VMEM((4, 4, HROWS, D), BF),
            pltpu.VMEM((4, 4, HROWS, D), BF),
            pltpu.VMEM((3, 4, HROWS, D), BF),
            pltpu.VMEM((3, HROWS, D), BF),
            pltpu.VMEM((4, HROWS, D), BF),
            pltpu.VMEM((HROWS, D), BF),
            pltpu.VMEM((2, 2, HROWS, D), BF),
            dma((4,)),
            dma((4,)),
            dma((4,)),
            dma((4,)),
            dma((4,)),
            dma((4,)),
            dma((4,)),
            dma((4,)),
            dma((2, 2)),
            dma((4,)),
            dma((2, 2)),
            dma((3,)),
        ],
        compiler_params=comm_params(5),
    )(grads, result, ingrad)


def halves_first(v, rows):
    return v.reshape(rows, 3, 2, HALF).transpose(0, 2, 1, 3).reshape(rows, 3 * D)


def thirds_first(v, rows):
    return v.reshape(rows, 2, 3, HALF).transpose(0, 2, 1, 3).reshape(rows, 3 * D)


def body(inputs, cotangent, w_qkv, w_out, w_fc, w_proj, gains, biases, fc_bias):
    def stacked(v, blocks):
        return v.reshape(48, blocks, D).transpose(1, 0, 2).reshape(48 * blocks, D)

    small = jnp.concatenate([gains.reshape(96), biases.reshape(288), fc_bias.reshape(192)])
    small = jnp.pad(small[None], ((0, 31), (0, D - 576)))
    shard = jnp.concatenate(
        [
            stacked(halves_first(w_qkv[0], 48), 3),
            w_out[0],
            stacked(w_fc[0], 4),
            w_proj[0],
            small,
        ],
        0,
    )
    full, stream = gather(shard, inputs, cotangent)
    full = full.reshape(16, ROWS, D)

    def lanes(v, rows):
        return v.reshape(16, rows, 48).transpose(1, 0, 2).reshape(rows, D)

    values = full[:, 576, :576].astype(F32)
    shifts = lanes(values[:, 96:384], 6)
    packed_shift = jnp.concatenate([shifts[1], jnp.zeros((D,), F32), shifts[2]])
    par = jnp.concatenate(
        [
            lanes(values[:, :96], 2),
            shifts,
            values[:, 384:].reshape(4, D),
            halves_first(packed_shift[None], 1).reshape(3, D),
            jnp.zeros((1, D), F32),
        ],
        0,
    )

    def forward(x, keep):
        packed, normed = front(x, full, par)
        heads = cross(packed, 1).reshape(L, 3 * HALF)
        mixed_heads, logs = attend(heads)
        mixed = cross(mixed_heads.reshape(2, T, HALF), 2)
        return rear(x, mixed, full, par, keep), (normed, heads, mixed_heads, logs, mixed)

    (made,), _ = forward(stream, False)
    x = hand_over(made, stream, 0)
    (result, middle, normed2, pre, active), (normed, heads, mixed_heads, logs, mixed) = forward(
        x, True
    )

    def backward(e):
        gmixed, gmiddle, mlow, gpre, rear_sums = rear_back(e, middle, pre, full, par)
        gheads = cross(gmixed, 2).reshape(L, HALF)
        gpacked = attend_back(heads, mixed_heads, gheads, logs)
        gp = cross(gpacked.reshape(2, T, 3 * HALF), 1)
        grad, front_sums = front_back(gp, gmiddle, x, full, par)
        return grad, gp, mlow, gpre, rear_sums, front_sums

    grad = backward(stream)[0]
    e = hand_over(grad, stream, 1)
    grad, gp, mlow, gpre, rear_sums, front_sums = backward(e)

    def shards(v, rows):
        return v.reshape(rows, 16, 48).transpose(1, 0, 2).reshape(16, rows * 48)

    packed_sums = thirds_first(front_sums[2:5].reshape(1, 3 * D), 1).reshape(3, D)
    small = jnp.concatenate(
        [
            shards(jnp.stack([front_sums[0], rear_sums[1]]), 2),
            shards(
                jnp.stack(
                    [
                        front_sums[1],
                        packed_sums[0],
                        packed_sums[2],
                        rear_sums[3],
                        rear_sums[2],
                        rear_sums[0],
                    ]
                ),
                6,
            ),
            rear_sums[4:8].reshape(16, 192),
        ],
        1,
    ).astype(BF)
    small = jnp.pad(small[:, None, :], ((0, 0), (0, 31), (0, D - 576)))
    grads = weight_grads(normed, gp, mixed, mlow, normed2, gpre, active, e, small)
    total, section_out, in_grad = reduce(grads.reshape(4, 4, ROWS, D), result, grad)

    def unstacked(v, blocks):
        return v.reshape(blocks, 48, D).transpose(1, 0, 2).reshape(48, blocks * D)

    tail = total[576, :576]
    return (
        section_out[None],
        in_grad[None],
        thirds_first(unstacked(total[:144], 3), 48)[None],
        total[144:192][None],
        unstacked(total[192:384], 4)[None],
        total[384:576][None],
        tail[:96].reshape(1, 2, 48),
        tail[96:384].reshape(1, 6, 48),
        tail[384:].reshape(1, 192),
    )


def solution(mesh):
    in_specs = (
        P("dp", "seq", None),
        P("dp", "seq", None),
        P("section", "dp", None),
        P("section", "dp", None),
        P("section", "dp", None),
        P("section", "dp", None),
        P("section", None, "dp"),
        P("section", None, "dp"),
        P("section", "dp"),
    )
    out_specs = (
        P("section", "dp", "seq", None),
        P("section", "dp", "seq", None),
        P("section", "dp", None),
        P("section", "dp", None),
        P("section", "dp", None),
        P("section", "dp", None),
        P("section", None, "dp"),
        P("section", None, "dp"),
        P("section", "dp"),
    )
    return jax.shard_map(body, mesh=mesh, in_specs=in_specs, out_specs=out_specs, check_vma=False)
```

time: 1330 us -> 641 us (0.48)
  Pallas kernels: 0 us -> 603 us
  waiting for transfers between devices: 560 us -> 0 us
  other arithmetic: 183 us -> 3.56 us
  blocking collectives: 137 us -> 0 us
  local copies, waits for them, and re-layouts: 156 us -> 22.4 us
  matrix products: 130 us -> 0 us
  starting transfers between devices: 98.8 us -> 0 us
  loops' own time: 40.7 us -> 0 us
  between operations: 16 us -> 1.46 us
    pallas_call x0 -> x25, Pallas kernels: none -> 603 us  [the longest x8 202 us: cross(): pl.pallas_call(cross_kernel, name='cross_cores', out_shape=jax.ShapeDtype...]
    reduce_scatter x4 -> x0, waiting for transfers between devices: 291 us -> none  [the longest x1 81.2 us: body(): lax.psum_scatter(lifted[2].astype(jnp.bfloat16), 'dp', scatter_dimension=...]
    dot_general x52 -> x0, matrix products: 130 us -> none  [the longest x2 15 us: rear_back(): grad_act = jnp.dot(grad_low, w_down.T, preferred_element_type=jnp.float32)]
    all_gather x4 -> x0, waiting for transfers between devices: 123 us -> none  [the longest x1 55.7 us: body(): lax.all_gather(w_fc, 'dp', axis=1, tiled=True)]
    add x27 -> x0, other arithmetic: 106 us -> none  [the longest x21 105 us: backward_tick(): sums = tuple((total + term for total, term in zip(sums, terms)))]
    unnamed x2 -> x0, blocking collectives: 92.8 us -> none
    all_to_all x12 -> x0, waiting for transfers between devices: 64 us -> none  [the longest x3 46.8 us: forward_tick(): lax.all_to_all(packed, 'seq', split_axis=2, concat_axis=0, tiled=True)]
    ppermute x6 -> x0, starting transfers between devices: 53 us -> none  [passed_along(): return lax.ppermute(block, axis, route)]
  transfers between devices with their start and end apart: 28 -> 0, of which waited for: 19 -> 0; matrix products, arithmetic and copies ran while one was open for 14% -> 0% of each run, Pallas kernels for 0% -> 0%
where the time goes in v1:
time: 641 us; the launch traced here: 630 us
  Pallas kernels  603 us (94%)
  local copies, waits for them, and re-layouts  22.4 us (3%)
    pallas_call x8, Pallas kernels, cross(): pl.pallas_call(cross_kernel, name='cross_cores', out_shape=jax.ShapeDtype...  202 us
    pallas_call x1, Pallas kernels, reduce(): pl.pallas_call(reduce_kernel, name='reduce_grads', out_shape=(jax.ShapeDt...  101 us
    pallas_call x1, Pallas kernels, gather(): pl.pallas_call(gather_kernel, name='gather_weights', out_shape=(jax.Shape...  98.5 us
    pallas_call x2, Pallas kernels, hand_over(): pl.pallas_call(functools.partial(hand_kernel, giver), name='hand_over', o...  44.3 us
    pallas_call x2, Pallas kernels, attend_back(): pl.pallas_call(attend_back_kernel, name='attend_back', grid=(3,), out_sha...  33.6 us
    pallas_call x2, Pallas kernels, rear_back(): pl.pallas_call(rear_back_kernel, name='rear_back', grid=(STEPS,), out_sha...  31.3 us
    pallas_call x2, Pallas kernels, rear(): pl.pallas_call(rear_kernel, name='rear', grid=(STEPS,), out_shape=tuple((...  25.7 us
    pallas_call x2, Pallas kernels, attend(): pl.pallas_call(attend_kernel, name='attend', grid=(3,), out_shape=(jax.Sh...  24 us

profile of v1, /device:TPU:1, one launch (start us, length us, event | category | flops | bytes accessed | tf_op | source)
XLA Modules:
  0.0 630.1 jit_solution(12619922316043074581)
XLA Ops:
  6.0 98.5 %gather_weights.1 = (bf16[4,4,608,768]{3,2,1,0:T(8,128)(2,1)}, bf16[512,768]{1,0:T(8,128)(2,1)}) custom-call(bf16[608,768]{1,0:T(8,128)(2,1)} %copy-done, bf16[2,256,768]{2,1,0:T(8,128)(2,1)} %ins.1, bf16[2,256,768]{2,1,0:T(8,128)(2,1)} %cots.1), custom_call_target="tpu_custom_call" | custom-call | tf_op jit(solution)/shard_map/gather_weights/pallas_call | solution.py:230
  106.2 1.3 concatenate.34.par
  107.5 5.9 front.2
  113.4 37.0 %cross_cores.8 = bf16[2,512,1152]{2,1,0:T(8,128)(2,1)} custom-call(bf16[2,512,1152]{2,1,0:T(8,128)(2,1)} %get-tuple-element.37.src), custom_call_target="tpu_custom_call" | custom-call | tf_op jit(solution)/shard_map/cross_cores/pallas_call | solution.py:264
  150.4 12.0 %attend.2 = (bf16[1024,384]{1,0:T(8,128)(2,1)}, f32[3,1024,128]{2,1,0:T(8,128)}) custom-call(bf16[1024,1152]{1,0:T(8,128)(2,1)} %bitcast.76, bf16[1024,1152]{1,0:T(8,128)(2,1)} %bitcast.77, bf16[1024,1152]{1,0:T(8,128)(2,1)} %bitcast.78), custom_call_target="tpu_custom_call" | custom-call | tf_op jit(solution)/shard_map/attend/pallas_call | solution.py:439
  162.4 13.4 %cross_cores.9.mixed = bf16[2,512,384]{2,1,0:T(8,128)(2,1)} custom-call(bf16[2,512,384]{2,1,0:T(8,128)(2,1)} %bitcast.94), custom_call_target="tpu_custom_call" | custom-call | tf_op jit(solution)/shard_map/cross_cores/pallas_call | solution.py:264
  175.8 12.2 %rear.2.made = bf16[512,768]{1,0:T(8,128)(2,1)} custom-call(bf16[512,768]{1,0:T(8,128)(2,1)} %get-tuple-element.35.x.held.e, bf16[2,512,384]{2,1,0:T(8,128)(2,1)} %cross_cores.9.mixed, bf16[16,608,768]{2,1,0:T(8,128)(2,1)} %bitcast.51, bf16[16,608,768]{2,1,0:T(8,128)(2,1)} %bitcast.52, bf16[16,608,768]{2,1,0:T(8,128)(2,1)} %bitcast.53, ...), custom_call_target="tpu_custom_call" | custom-call | tf_op jit(solution)/shard_map/rear/pallas_call | solution.py:548
  188.0 25.0 %hand_over.2.x = bf16[512,768]{1,0:T(8,128)(2,1)} custom-call(bf16[512,768]{1,0:T(8,128)(2,1)} %rear.2.made, bf16[512,768]{1,0:T(8,128)(2,1)} %get-tuple-element.35.x.held.e), custom_call_target="tpu_custom_call" | custom-call | tf_op jit(solution)/shard_map/hand_over/pallas_call | solution.py:295
  212.9 5.9 front.3
  218.9 37.0 %cross_cores.10 = bf16[2,512,1152]{2,1,0:T(8,128)(2,1)} custom-call(bf16[2,512,1152]{2,1,0:T(8,128)(2,1)} %get-tuple-element.40.src), custom_call_target="tpu_custom_call" | custom-call | tf_op jit(solution)/shard_map/cross_cores/pallas_call | solution.py:264
  255.9 12.0 %attend.3 = (bf16[1024,384]{1,0:T(8,128)(2,1)}, f32[3,1024,128]{2,1,0:T(8,128)}) custom-call(bf16[1024,1152]{1,0:T(8,128)(2,1)} %bitcast.66, bf16[1024,1152]{1,0:T(8,128)(2,1)} %bitcast.67, bf16[1024,1152]{1,0:T(8,128)(2,1)} %bitcast.68), custom_call_target="tpu_custom_call" | custom-call | tf_op jit(solution)/shard_map/attend/pallas_call | solution.py:439
  267.9 13.4 %cross_cores.11.mixed = bf16[2,512,384]{2,1,0:T(8,128)(2,1)} custom-call(bf16[2,512,384]{2,1,0:T(8,128)(2,1)} %bitcast.81), custom_call_target="tpu_custom_call" | custom-call | tf_op jit(solution)/shard_map/cross_cores/pallas_call | solution.py:264
  281.3 13.5 %rear.3 = (bf16[512,768]{1,0:T(8,128)(2,1)}, f32[512,768]{1,0:T(8,128)}, bf16[512,768]{1,0:T(8,128)(2,1)}, bf16[512,3072]{1,0:T(8,128)(2,1)}, bf16[512,3072]{1,0:T(8,128)(2,1)}) custom-call(bf16[512,768]{1,0:T(8,128)(2,1)} %hand_over.2.x, bf16[2,512,384]{2,1,0:T(8,128)(2,1)} %cross_cores.11.mixed, bf16[16,608,768]{2,1,0:T(8,128)(2,1)} %bitcast.55, ...), custom_call_target="tpu_custom_call" | custom-call | tf_op jit(solution)/shard_map/rear/pallas_call | solution.py:548
  294.8 15.6 %rear_back.2 = (bf16[2,512,384]{2,1,0:T(8,128)(2,1)}, f32[512,768]{1,0:T(8,128)}, bf16[512,768]{1,0:T(8,128)(2,1)}, bf16[512,3072]{1,0:T(8,128)(2,1)}, f32[8,768]{1,0:T(8,128)}) custom-call(bf16[512,768]{1,0:T(8,128)(2,1)} %get-tuple-element.35.x.held.e, f32[512,768]{1,0:T(8,128)} %get-tuple-element.42.middle, bf16[512,3072]{1,0:T(8,128)(2,1)} %get-tuple-element.43.pre, ...), custom_call_target="tpu_custom_call" | custom-call | tf_op jit(solution)/shard_map/rear_back/pallas_call | solution.py:601
  310.4 13.3 %cross_cores.12 = bf16[2,512,384]{2,1,0:T(8,128)(2,1)} custom-call(bf16[2,512,384]{2,1,0:T(8,128)(2,1)} %get-tuple-element.44.src), custom_call_target="tpu_custom_call" | custom-call | tf_op jit(solution)/shard_map/cross_cores/pallas_call | solution.py:264
  323.7 16.8 %attend_back.2 = bf16[1024,1152]{1,0:T(8,128)(2,1)} custom-call(bf16[1024,1152]{1,0:T(8,128)(2,1)} %bitcast.69, bf16[1024,1152]{1,0:T(8,128)(2,1)} %bitcast.70, bf16[1024,1152]{1,0:T(8,128)(2,1)} %bitcast.71, bf16[1024,384]{1,0:T(8,128)(2,1)} %get-tuple-element.41.o_ref, bf16[1024,384]{1,0:T(8,128)(2,1)} %bitcast.83, f32[3,1024,128]{2,1,0:T(8,128)} %get-tuple-element.45.logs), custom_call_target="tpu_custom_call" | custom-call | tf_op jit(solution)/shard_map/attend_back/pallas_call | solution.py:492
  340.5 37.2 %cross_cores.13.gp = bf16[2,512,1152]{2,1,0:T(8,128)(2,1)} custom-call(bf16[2,512,1152]{2,1,0:T(8,128)(2,1)} %bitcast.80), custom_call_target="tpu_custom_call" | custom-call | tf_op jit(solution)/shard_map/cross_cores/pallas_call | solution.py:264
  377.8 6.5 %front_back.2 = (bf16[512,768]{1,0:T(8,128)(2,1)}, f32[8,768]{1,0:T(8,128)}) custom-call(bf16[2,512,1152]{2,1,0:T(8,128)(2,1)} %cross_cores.13.gp, f32[512,768]{1,0:T(8,128)} %get-tuple-element.46.gmiddle, bf16[512,768]{1,0:T(8,128)(2,1)} %hand_over.2.x, bf16[16,608,768]{2,1,0:T(8,128)(2,1)} %bitcast.61, f32[16,768]{1,0:T(8,128)} %concatenate.34.par), custom_call_target="tpu_custom_call" | custom-call | tf_op jit(solution)/shard_map/front_back/pallas_call | solution.py:651
  384.3 19.3 %hand_over.3.e.top = bf16[512,768]{1,0:T(8,128)(2,1)} custom-call(bf16[512,768]{1,0:T(8,128)(2,1)} %get-tuple-element.47.made, bf16[512,768]{1,0:T(8,128)(2,1)} %get-tuple-element.35.x.held.e), custom_call_target="tpu_custom_call" | custom-call | tf_op jit(solution)/shard_map/hand_over/pallas_call | solution.py:295
  403.6 15.7 %rear_back.3 = (bf16[2,512,384]{2,1,0:T(8,128)(2,1)}, f32[512,768]{1,0:T(8,128)}, bf16[512,768]{1,0:T(8,128)(2,1)}, bf16[512,3072]{1,0:T(8,128)(2,1)}, f32[8,768]{1,0:T(8,128)}) custom-call(bf16[512,768]{1,0:T(8,128)(2,1)} %hand_over.3.e.top, f32[512,768]{1,0:T(8,128)} %get-tuple-element.42.middle, bf16[512,3072]{1,0:T(8,128)(2,1)} %get-tuple-element.43.pre, ...), custom_call_target="tpu_custom_call" | custom-call | tf_op jit(solution)/shard_map/rear_back/pallas_call | solution.py:601
  419.3 14.1 %cross_cores.14 = bf16[2,512,384]{2,1,0:T(8,128)(2,1)} custom-call(bf16[2,512,384]{2,1,0:T(8,128)(2,1)} %get-tuple-element.48.src), custom_call_target="tpu_custom_call" | custom-call | tf_op jit(solution)/shard_map/cross_cores/pallas_call | solution.py:264
  433.4 16.8 %attend_back.3 = bf16[1024,1152]{1,0:T(8,128)(2,1)} custom-call(bf16[1024,1152]{1,0:T(8,128)(2,1)} %bitcast.72, bf16[1024,1152]{1,0:T(8,128)(2,1)} %bitcast.73, bf16[1024,1152]{1,0:T(8,128)(2,1)} %bitcast.74, bf16[1024,384]{1,0:T(8,128)(2,1)} %get-tuple-element.41.o_ref, bf16[1024,384]{1,0:T(8,128)(2,1)} %bitcast.82, f32[3,1024,128]{2,1,0:T(8,128)} %get-tuple-element.45.logs), custom_call_target="tpu_custom_call" | custom-call | tf_op jit(solution)/shard_map/attend_back/pallas_call | solution.py:492
  450.2 36.9 %cross_cores.15.gp = bf16[2,512,1152]{2,1,0:T(8,128)(2,1)} custom-call(bf16[2,512,1152]{2,1,0:T(8,128)(2,1)} %bitcast.79), custom_call_target="tpu_custom_call" | custom-call | tf_op jit(solution)/shard_map/cross_cores/pallas_call | solution.py:264
  487.1 6.5 %front_back.3 = (bf16[512,768]{1,0:T(8,128)(2,1)}, f32[8,768]{1,0:T(8,128)}) custom-call(bf16[2,512,1152]{2,1,0:T(8,128)(2,1)} %cross_cores.15.gp, f32[512,768]{1,0:T(8,128)} %get-tuple-element.53.gmiddle, bf16[512,768]{1,0:T(8,128)(2,1)} %hand_over.2.x, bf16[16,608,768]{2,1,0:T(8,128)(2,1)} %bitcast.65, f32[16,768]{1,0:T(8,128)} %concatenate.34.par), custom_call_target="tpu_custom_call" | custom-call | tf_op jit(solution)/shard_map/front_back/pallas_call | solution.py:651
  496.2 1.1 fusion.8.small
  497.3 17.6 %weight_grads.1 = bf16[16,608,768]{2,1,0:T(8,128)(2,1)} custom-call(bf16[512,768]{1,0:T(8,128)(2,1)} %get-tuple-element.39.normed, bf16[2,512,1152]{2,1,0:T(8,128)(2,1)} %cross_cores.15.gp, bf16[2,512,384]{2,1,0:T(8,128)(2,1)} %cross_cores.11.mixed, bf16[512,768]{1,0:T(8,128)(2,1)} %get-tuple-element.49.mlow, bf16[512,768]{1,0:T(8,128)(2,1)} %get-tuple-element.50.normed2, ...), custom_call_target="tpu_custom_call" | custom-call | tf_op jit(solution)/shard_map/weight_grads/pallas_call | solution.py:687
  514.9 100.7 %reduce_grads.1 = (f32[608,768]{1,0:T(8,128)}, bf16[2,256,768]{2,1,0:T(8,128)(2,1)}, bf16[2,256,768]{2,1,0:T(8,128)(2,1)}) custom-call(bf16[4,4,608,768]{3,2,1,0:T(8,128)(2,1)} %bitcast.75, bf16[512,768]{1,0:T(8,128)(2,1)} %get-tuple-element.56.result, bf16[512,768]{1,0:T(8,128)(2,1)} %get-tuple-element.57.ingrad), custom_call_target="tpu_custom_call" | custom-call | tf_op jit(solution)/shard_map/reduce_grads/pallas_call | solution.py:865
  616.9 1.3 slice.111
  619.6 1.6 slice_bitcast_fusion.1
  622.2 2.1 slice_bitcast_fusion
  624.8 1.1 broadcast_in_dim_reshape.7
  626.9 1.1 broadcast_in_dim_reshape.6
  (88 shorter events, 16.4 us)
Async XLA Ops:
  0.6 3.8 copy-start.3
  0.7 4.1 copy-start.5
  4.0 1.0 copy-start.4
  5.0 0.9 copy-start
  487.0 8.3 %copy-start.6 = (f32[8,768]{1,0:T(8,128)S(1)}, f32[8,768]{1,0:T(8,128)}, u32[]{:S(2)}) copy-start(f32[8,768]{1,0:T(8,128)} %get-tuple-element.55) | copy-start | bytes 73732
  625.9 2.1 copy-start.2
  626.6 2.2 copy-start.1

commit v2 on v1

v2 whole, which is shorter than its diff:
```python
import functools
import math

import jax
import jax.numpy as jnp
from jax import lax
from jax.experimental import pallas as pl
from jax.experimental.pallas import tpu as pltpu
from jax.sharding import PartitionSpec as P

MESH = pl.DeviceIdType.MESH
BF = jnp.bfloat16
F32 = jnp.float32
D = 768
T = 512
L = 1024
HALF = 384
ROWS = 608
HROWS = ROWS // 2
EPS = 1e-05
FC_ROWS = (192, 240, 304, 352)
SCALE = 0.125
C2 = SCALE * math.log2(math.e)
VLIM = 60 * 1024 * 1024
ANY = pl.BlockSpec(memory_space=pl.ANY)
VM = pl.BlockSpec(memory_space=pltpu.VMEM)


def where_am_i():
    core = lax.axis_index("section")
    z = lax.axis_index("seq")
    dp = lax.axis_index("dp")
    return core, z, dp // 4, dp % 4


def greet(peers):
    barrier = pltpu.get_barrier_semaphore()
    for peer in peers:
        pl.semaphore_signal(barrier, inc=1, device_id=peer, device_id_type=MESH)
    pl.semaphore_wait(barrier, len(peers))


def remote(src, dst, send, recv, peer):
    return pltpu.make_async_remote_copy(
        src_ref=src, dst_ref=dst, send_sem=send, recv_sem=recv, device_id=peer, device_id_type=MESH
    )


def comm_params(ident):
    return pltpu.CompilerParams(
        collective_id=ident, has_side_effects=True, vmem_limit_bytes=VLIM
    )


PIECES = ((0, 96), (96, 96), (192, 112))


def gather_kernel(
    wq, wo, wf, wp, small, ins, cots, full, stream, shard, part, lsem, gs, gr, ssem, rsem, xs, xr
):
    core, z, y, x = where_am_i()
    block = z % 2
    sib = 1 - core
    dp = y * 4 + x
    sibling = (sib, z, dp)
    first = core == 0
    count = len(PIECES)

    def along(axis, step):
        if axis == 0:
            return (core, z, y * 4 + (x + step) % 4)
        return (core, z, ((y + step) % 4) * 4 + x)

    @pl.when(core == block)
    def _():
        for h in range(2):
            for k in range(3):
                at = h * 3 + k
                shard[(at // 2) * 48 : (at // 2 + 1) * 48, (at % 2) * HALF : (at % 2 + 1) * HALF] = (
                    wq[0, :, k * D + h * HALF : k * D + (h + 1) * HALF]
                )
        shard[144:192] = wo[0]
        for m in range(4):
            shard[FC_ROWS[m] : FC_ROWS[m] + 48] = wf[0, :, m * D : (m + 1) * D]
        shard[288:304] = small[...]
        shard[400:592] = wp[0]
        shard[592:608] = jnp.zeros((16, D), BF)

    peers = [sibling]
    for step in (1, 2, 3):
        peers += [along(0, step), along(1, step), (core, (z + step) % 4, dp)]
    greet(peers)

    def span(p, whose):
        at, rows = PIECES[p]
        return pl.ds(pl.multiple_of(whose * HROWS + at, 16), rows)

    def give(p):
        view = shard.at[span(p, sib)]
        return remote(view, view, gs.at[p], gr.at[p], sibling)

    @pl.when(core == block)
    def _():
        for p in range(count):
            give(p).start()

    quarter = pl.ds(pl.multiple_of((z % 2) * 256, 256), 256)
    sends_tokens = (z // 2) == core
    for step in (1, 2, 3):
        to = (z + step) % 4
        for source, parity in ((ins, 0), (cots, 1)):

            @pl.when(sends_tokens & (to % 2 == parity))
            def _():
                remote(
                    source.at[to // 2],
                    stream.at[quarter],
                    xs.at[step],
                    xr.at[z % 2],
                    (core, to, dp),
                ).start()

    for source, parity in ((ins, 0), (cots, 1)):

        @pl.when(sends_tokens & (z % 2 == parity))
        def _():
            pltpu.make_async_copy(source.at[z // 2], part, lsem.at[count]).start()

    def shard_at(p, axis, step, whose):
        rows = span(p, whose)
        if axis == 0:
            return full.at[y, (x + step) % 4, rows]
        return full.at[(y + step) % 4, x, rows]

    def line_at(p, axis, step, half, whose):
        rows = span(p, whose)
        if axis == 0:
            return full.at[pl.ds(2 * half, 2), (x + step) % 4, rows]
        return full.at[(y + step) % 4, pl.ds(2 * half, 2), rows]

    def rest(axis):
        cross = 1 - axis
        out = []

        def send(p, slot, src, dst, to):
            copy = remote(src, dst, ssem.at[p, slot], rsem.at[p, slot], to)
            copy.start()
            out.append(copy)

        def came(p, slot, land):
            remote(land, land, ssem.at[p, slot], rsem.at[p, slot], sibling).wait_recv()

        for p in range(count):

            @pl.when(core != block)
            def _():
                view = shard.at[span(p, core)]
                remote(view, view, gs.at[p], gr.at[p], sibling).wait_recv()

            view = shard.at[span(p, core)]
            land = shard_at(p, axis, 0, core)
            for k in (2, 1, 3):
                send(p, k, view, land, along(axis, k))
            send(p, 14, view, land, sibling)
            pltpu.make_async_copy(view, land, lsem.at[p]).start()
        for p in range(count):
            land = shard_at(p, axis, 0, core)
            pltpu.make_async_copy(shard.at[span(p, core)], land, lsem.at[p]).wait()
            for k in (1, 3, 2):
                came(p, k, shard_at(p, axis, 4 - k, core))
            for half in (0, 1):
                for slot, step in ((4, 1), (6, 3)):
                    view = line_at(p, cross, 0, half, core)
                    send(p, slot + half, view, view, along(cross, step))
            for k in (1, 3, 2):
                view = shard_at(p, axis, 4 - k, core)
                send(p, 14 + k, view, view, sibling)
        for p in range(count):
            for half, slot, step, to in ((0, 4, 3, 1), (1, 6, 1, 3), (1, 4, 3, 0), (0, 6, 1, 0)):
                land = line_at(p, cross, step, half, core)
                came(p, slot + half, land)
                if to:
                    send(p, 8 + half, land, land, along(cross, to))
                send(p, 14 + slot + half, land, land, sibling)
        for p in range(count):
            for half in (0, 1):
                land = line_at(p, cross, 2, half, core)
                came(p, 8 + half, land)
                send(p, 22 + half, land, land, sibling)
        for p in range(count):
            came(p, 14, shard_at(p, cross, 0, sib))
            for k in (1, 3, 2):
                came(p, 14 + k, shard_at(p, cross, 4 - k, sib))
            for half, slot, step in ((0, 4, 3), (1, 6, 1), (1, 4, 3), (0, 6, 1)):
                came(p, 14 + slot + half, line_at(p, axis, step, half, sib))
            for half in (0, 1):
                came(p, 22 + half, line_at(p, axis, 2, half, sib))
        for copy in out:
            copy.wait_send()

    @pl.when(first)
    def _():
        rest(0)

    @pl.when(jnp.logical_not(first))
    def _():
        rest(1)

    @pl.when(core == block)
    def _():
        for p in range(count):
            give(p).wait_send()

    @pl.when(sends_tokens)
    def _():
        pltpu.make_async_copy(ins.at[0], part, lsem.at[count]).wait()
        copy = pltpu.make_async_copy(part, stream.at[quarter], lsem.at[count])
        copy.start()
        for step in (1, 2, 3):
            remote(ins.at[0], stream.at[quarter], xs.at[step], xr.at[0], sibling).wait_send()
        copy.wait()

    for j in (0, 1):

        @pl.when(z != 2 * core + j)
        def _():
            land = stream.at[pl.ds(256 * j, 256)]
            remote(land, land, xs.at[0], xr.at[j], sibling).wait_recv()


def gather(wq, wo, wf, wp, small, ins, cots):
    dma = pltpu.SemaphoreType.DMA
    n = len(PIECES)
    return pl.pallas_call(
        gather_kernel,
        name="gather_weights",
        out_shape=(
            jax.ShapeDtypeStruct((4, 4, ROWS, D), BF),
            jax.ShapeDtypeStruct((T, D), BF),
        ),
        in_specs=[VM] * 5 + [ANY] * 2,
        out_specs=(ANY, ANY),
        scratch_shapes=[
            pltpu.VMEM((ROWS, D), BF),
            pltpu.VMEM((256, D), BF),
            dma((n + 1,)),
            dma((n,)),
            dma((n,)),
            dma((n, 24)),
            dma((n, 24)),
            dma((4,)),
            dma((2,)),
        ],
        compiler_params=comm_params(0),
    )(wq, wo, wf, wp, small, ins, cots)


def cross_kernel(src, dst, stage, lsem, ssem, rsem):
    core, z, y, x = where_am_i()
    sibling = (1 - core, z, y * 4 + x)
    local_in = pltpu.make_async_copy(src.at[core], stage, lsem)
    local_in.start()
    greet([sibling])
    out = remote(src.at[1 - core], dst.at[core], ssem, rsem, sibling)
    out.start()
    local_in.wait()
    local_out = pltpu.make_async_copy(stage, dst.at[core], lsem)
    local_out.start()
    local_out.wait()
    out.wait_send()
    remote(src.at[1 - core], dst.at[1 - core], ssem, rsem, sibling).wait_recv()


def cross(pieces, ident):
    return pl.pallas_call(
        cross_kernel,
        name="cross_cores",
        out_shape=jax.ShapeDtypeStruct(pieces.shape, pieces.dtype),
        in_specs=[ANY],
        out_specs=ANY,
        scratch_shapes=[pltpu.VMEM(pieces.shape[1:], pieces.dtype)]
        + [pltpu.SemaphoreType.DMA] * 3,
        compiler_params=comm_params(ident),
    )(pieces)


def dot(a, b):
    return jnp.dot(a, b, preferred_element_type=F32)


def dot_nt(a, b):
    return lax.dot_general(a, b, (((1,), (1,)), ((), ())), preferred_element_type=F32)


def dot_tn(a, b):
    return lax.dot_general(a, b, (((0,), (0,)), ((), ())), preferred_element_type=F32)


def normalized(v):
    centre = v - jnp.mean(v, axis=-1, keepdims=True)
    inv = lax.rsqrt(jnp.mean(centre * centre, axis=-1, keepdims=True) + EPS)
    return centre * inv, inv


def norm_back(grad, gain, unit, inv):
    g = grad * gain
    return inv * (
        g
        - jnp.mean(g, axis=-1, keepdims=True)
        - unit * jnp.mean(g * unit, axis=-1, keepdims=True)
    )


def matrix(ref, m):
    return ref[m].reshape(D, D)


class Fetch:
    def __init__(self, w, sems, parts):
        self.copies = []
        for at, (buffer, m, kind) in enumerate(parts):
            if kind is None:
                src = w.at[pl.ds(4 * m, 4), pl.ds(400, 192)]
            else:
                src = w.at[:, pl.ds(kind, 48)]
            self.copies.append(pltpu.make_async_copy(src, buffer.at[m], sems.at[at]))
        for copy in self.copies:
            copy.start()

    def need(self, at):
        self.copies[at].wait()


class Store:
    def __init__(self, sems):
        self.sems = sems
        self.copies = []

    def put(self, src, dst):
        copy = pltpu.make_async_copy(src, dst, self.sems.at[len(self.copies)])
        copy.start()
        self.copies.append(copy)

    def finish(self):
        for copy in self.copies:
            copy.wait()


def wide(*lead):
    return pltpu.VMEM((*lead, D), BF)


def local_params():
    return pltpu.CompilerParams(vmem_limit_bytes=VLIM)


TILES = (slice(0, 256), slice(256, 512))


def front_tile(at, need, x, wq, par, packed, normed_out):
    unit, _ = normalized(x[at].astype(F32))
    normed = (unit * par[0:1] + par[2:3]).astype(BF)
    normed_out[at] = normed
    need(0)
    a = (dot(normed, matrix(wq, 0)) + par[12:13]).astype(BF)
    packed[0, at, :D] = a
    need(1)
    b = (dot(normed, matrix(wq, 1)) + par[13:14]).astype(BF)
    packed[0, at, D:] = b[:, :HALF]
    packed[1, at, :HALF] = b[:, HALF:]
    need(2)
    c = (dot(normed, matrix(wq, 2)) + par[14:15]).astype(BF)
    packed[1, at, HALF:] = c


def nothing(at):
    pass


def front_kernel(x, w, par, packed, normed_out, wq, sems):
    fetch = Fetch(w, sems, QKV_PARTS(wq))
    for i, at in enumerate(TILES):
        front_tile(at, nothing if i else fetch.need, x, wq, par, packed, normed_out)


def QKV_PARTS(wq):
    return [(wq, m, 48 * m) for m in range(3)]


def front(x, w, par):
    return pl.pallas_call(
        front_kernel,
        name="front",
        out_shape=(
            jax.ShapeDtypeStruct((2, T, 3 * HALF), BF),
            jax.ShapeDtypeStruct((T, D), BF),
        ),
        in_specs=[VM, ANY, VM],
        out_specs=(VM, VM),
        scratch_shapes=[wide(3, 16, 48), pltpu.SemaphoreType.DMA((3,))],
        compiler_params=local_params(),
    )(x, w, par)


QB = 256


def head_masks(ref_value):
    lane = lax.broadcasted_iota(jnp.int32, ref_value.shape, 1)
    zero = jnp.zeros_like(ref_value)
    return (
        jnp.where(lane < 64, ref_value, zero),
        jnp.where(lane >= 64, ref_value, zero),
    )


def causal(rows, cols, offset):
    row = lax.broadcasted_iota(jnp.int32, (rows, cols), 0) + offset
    return lax.broadcasted_iota(jnp.int32, (rows, cols), 1) <= row


def attend_kernel(q_ref, k_ref, v_ref, mixed, logs):
    for i in range(L // QB):
        at = slice(i * QB, (i + 1) * QB)
        stop = (i + 1) * QB
        keys = k_ref[:stop]
        queries = head_masks(q_ref[at])
        values = head_masks(v_ref[:stop])
        keep = causal(QB, stop, i * QB)
        total = None
        saved = []
        for h in range(2):
            s = jnp.where(keep, dot_nt(queries[h], keys), -1e30)
            peak = jnp.max(s, axis=-1, keepdims=True)
            p = jnp.exp2((s - peak) * C2)
            norm = jnp.sum(p, axis=-1, keepdims=True)
            o = dot(p.astype(BF), values[h]) * (1.0 / norm)
            total = o if total is None else total + o
            saved.append(peak * C2 + jnp.log2(norm))
        mixed[at] = total.astype(BF)
        lane = lax.broadcasted_iota(jnp.int32, (QB, 128), 1)
        logs[0, at] = jnp.where(lane < 64, saved[0], saved[1])


def attend(heads):
    def col(k):
        return pl.BlockSpec((L, 128), lambda p: (0, p + 3 * k))

    return pl.pallas_call(
        attend_kernel,
        name="attend",
        grid=(3,),
        out_shape=(
            jax.ShapeDtypeStruct((L, HALF), BF),
            jax.ShapeDtypeStruct((3, L, 128), F32),
        ),
        in_specs=[col(0), col(1), col(2)],
        out_specs=(col(0), pl.BlockSpec((1, L, 128), lambda p: (p, 0, 0))),
        compiler_params=local_params(),
    )(heads, heads, heads)


def attend_back_kernel(q_ref, k_ref, v_ref, o_ref, do_ref, logs, out, dk, dv):
    p_at = pl.program_id(0)
    dk[...] = jnp.zeros_like(dk)
    dv[...] = jnp.zeros_like(dv)

    def columns(part):
        return pl.ds(pl.multiple_of(part * HALF + p_at * 128, 128), 128)

    for i in range(L // QB):
        at = slice(i * QB, (i + 1) * QB)
        stop = (i + 1) * QB
        keys = k_ref[:stop]
        values = v_ref[:stop]
        keys_of = head_masks(keys)
        queries = head_masks(q_ref[at])
        tops = head_masks(do_ref[at])
        keep = causal(QB, stop, i * QB)
        inner = head_masks(do_ref[at].astype(F32) * o_ref[at].astype(F32))
        dq = None
        for h in range(2):
            s = dot_nt(queries[h], keys)
            total = logs[0, at, 64 * h : 64 * h + 1]
            p = jnp.where(keep, jnp.exp2(s * C2 - total), 0.0)
            gw = dot_nt(tops[h], values)
            delta = jnp.sum(inner[h], axis=-1, keepdims=True)
            ds = (p * (gw - delta)).astype(BF)
            part = dot(ds, keys_of[h])
            dq = part if dq is None else dq + part
            dk[:stop] += dot_tn(ds, queries[h])
            dv[:stop] += dot_tn(p.astype(BF), tops[h])
        out[at, columns(0)] = (dq * SCALE).astype(BF)
    out[:, columns(1)] = (dk[...] * SCALE).astype(BF)
    out[:, columns(2)] = dv[...].astype(BF)


def attend_back(heads, mixed, grad_mixed, logs):
    def col(k):
        return pl.BlockSpec((L, 128), lambda p: (0, p + 3 * k))

    return pl.pallas_call(
        attend_back_kernel,
        name="attend_back",
        grid=(3,),
        out_shape=jax.ShapeDtypeStruct((L, 3 * HALF), BF),
        in_specs=[
            col(0),
            col(1),
            col(2),
            col(0),
            col(0),
            pl.BlockSpec((1, L, 128), lambda p: (p, 0, 0)),
        ],
        out_specs=pl.BlockSpec((L, 3 * HALF), lambda p: (0, 0)),
        scratch_shapes=[pltpu.VMEM((L, 128), F32)] * 2,
        compiler_params=local_params(),
    )(heads, heads, heads, mixed, grad_mixed, logs)


REAR_SCRATCH = [
    wide(1, 16, 48),
    wide(4, 16, 48),
    wide(4, 4, 192),
    pltpu.SemaphoreType.DMA((9,)),
]


def gelu(v):
    return 0.5 * v * (1.0 + jnp.tanh(0.79788456 * (v + 0.044715 * v * v * v)))


def gelu_slope(v):
    square = v * v
    t = jnp.tanh(0.79788456 * v * (1.0 + 0.044715 * square))
    return 0.5 * (1.0 + t) + 0.5 * v * (1.0 - t * t) * 0.79788456 * (
        1.0 + 3 * 0.044715 * square
    )


def forward_parts(wo, wf, wp):
    parts = [(wo, 0, 144)]
    for m in range(4):
        parts += [(wf, m, FC_ROWS[m]), (wp, m, None)]
    return parts


def backward_parts(wo, wf, wp):
    parts = []
    for m in range(4):
        parts += [(wp, m, None), (wf, m, FC_ROWS[m])]
    return parts + [(wo, 0, 144)]


def rear_tile(at, need, x, mixed, wo, wf, wp, par, result, kept, store):
    mix = jnp.concatenate([mixed[0, at], mixed[1, at]], axis=1)
    need(0)
    middle = x[at].astype(F32) + (dot(mix, matrix(wo, 0)) + par[5:6])
    unit, _ = normalized(middle)
    normed = (unit * par[1:2] + par[6:7]).astype(BF)
    if kept:
        kept[0][at] = middle
        kept[1][at] = normed
        store(0, at, None)
        store(1, at, None)
    total = middle + par[7:8]
    for m in range(4):
        need(1 + 2 * m)
        pre = dot(normed, matrix(wf, m)) + par[8 + m : 9 + m]
        active = gelu(pre).astype(BF)
        if kept:
            cols = slice(m * D, (m + 1) * D)
            kept[2][at, cols] = pre.astype(BF)
            kept[3][at, cols] = active
            store(2, at, cols)
            store(3, at, cols)
        need(2 + 2 * m)
        total = total + dot(active, matrix(wp, m))
    result[at] = total.astype(BF)


def column_sum(v):
    return jnp.sum(v, axis=0, keepdims=True)


def adder(sums, i):
    def add(row, v):
        if i:
            sums[row : row + 1] += column_sum(v)
        else:
            sums[row : row + 1] = column_sum(v)

    return add


def rear_back_tile(at, need, e, middle, pre, wo, wf, wp, par, gmixed, gmiddle, full):
    if full:
        add, mlow, gpre, store = full
    top = e[at]
    gnorm = None
    for m in range(4):
        cols = slice(m * D, (m + 1) * D)
        need(2 * m)
        gact = dot_nt(top, matrix(wp, m))
        low = (gact * gelu_slope(pre[at, cols].astype(F32))).astype(BF)
        if full:
            gpre[at, cols] = low
            store(0, at, cols)
            add(4 + m, low.astype(F32))
        need(2 * m + 1)
        part = dot_nt(low, matrix(wf, m))
        gnorm = part if gnorm is None else gnorm + part
    unit, inv = normalized(middle[at])
    top_wide = top.astype(F32)
    gmid = top_wide + norm_back(gnorm, par[1:2], unit, inv)
    gmiddle[at] = gmid
    low = gmid.astype(BF)
    if full:
        add(0, top_wide)
        add(1, gnorm * unit)
        add(2, gnorm)
        add(3, gmid)
        mlow[at] = low
        store(1, at, None)
    need(8)
    gm = dot_nt(low, matrix(wo, 0)).astype(BF)
    gmixed[0, at] = gm[:, :HALF]
    gmixed[1, at] = gm[:, HALF:]


def front_back_tile(at, need, gp, gmiddle, x, wq, par, grad, add):
    gnorm = None
    for m, piece in enumerate(packed_pieces(gp, at)):
        if add:
            add(2 + m, piece.astype(F32))
        need(m)
        part = dot_nt(piece, matrix(wq, m))
        gnorm = part if gnorm is None else gnorm + part
    unit, inv = normalized(x[at].astype(F32))
    if add:
        add(0, gnorm * unit)
        add(1, gnorm)
    grad[at] = (gmiddle[at] + norm_back(gnorm, par[0:1], unit, inv)).astype(BF)


def partner_of():
    core, z, y, x = where_am_i()
    return z % 2, (core, z + 1 - 2 * (z % 2), y * 4 + x)


def rear_front_kernel(
    x, mixed, w, par, x2, packed, normed, wo, wf, wp, sems, wq, qsems, res, ssem, rsem
):
    block, partner = partner_of()
    fetch = Fetch(w, sems, forward_parts(wo, wf, wp))
    fetch_q = Fetch(w, qsems, QKV_PARTS(wq))
    greet([partner])

    def hand(i):
        rows = pl.ds(256 * i, 256)
        return remote(res.at[rows], x2.at[rows], ssem.at[i], rsem.at[i], partner)

    @pl.when(block == 0)
    def _():
        for i, at in enumerate(TILES):
            rear_tile(
                at, nothing if i else fetch.need, x, mixed, wo, wf, wp, par, res, None, None
            )
            hand(i).start()
        x2[...] = x[...]

    @pl.when(block == 1)
    def _():
        for k in range(9):
            fetch.need(k)

    for k in range(3):
        fetch_q.need(k)
    for i, at in enumerate(TILES):
        pl.when(block == 1)(hand(i).wait_recv)
        front_tile(at, nothing, x2, wq, par, packed, normed)

    @pl.when(block == 0)
    def _():
        for i in range(2):
            hand(i).wait_send()


def rear_front(x, mixed, w, par):
    dma = pltpu.SemaphoreType.DMA
    return pl.pallas_call(
        rear_front_kernel,
        name="rear_hand_front",
        out_shape=(
            jax.ShapeDtypeStruct((T, D), BF),
            jax.ShapeDtypeStruct((2, T, 3 * HALF), BF),
            jax.ShapeDtypeStruct((T, D), BF),
        ),
        in_specs=[VM, VM, ANY, VM],
        out_specs=(VM, VM, VM),
        scratch_shapes=REAR_SCRATCH
        + [wide(3, 16, 48), dma((3,)), wide(T), dma((2,)), dma((2,))],
        compiler_params=comm_params(3),
    )(x, mixed, w, par)


def turn_kernel(
    x, mixed, e, w, par, result, gmixed, gmiddle, middle_out, normed_out, pre_out, active_out,
    wo, wf, wp, sems, middle, normed, pre, active, osems,
):
    fetch = Fetch(w, sems, forward_parts(wo, wf, wp))
    store = Store(osems)
    kept = (middle, normed, pre, active)
    outs = (middle_out, normed_out, pre_out, active_out)

    def put(n, at, cols):
        rows = pl.ds(at.start, at.stop - at.start)
        if cols is None:
            store.put(kept[n].at[rows], outs[n].at[rows])
        else:
            lanes = pl.ds(cols.start, D)
            store.put(kept[n].at[rows, lanes], outs[n].at[rows, lanes])

    for i, at in enumerate(TILES):
        rear_tile(
            at, nothing if i else fetch.need, x, mixed, wo, wf, wp, par, result, kept, put
        )
    for at in TILES:
        rear_back_tile(at, nothing, e, middle, pre, wo, wf, wp, par, gmixed, gmiddle, None)
    store.finish()


def turn(x, mixed, e, w, par):
    kept = [((T, D), F32), ((T, D), BF), ((T, 4 * D), BF), ((T, 4 * D), BF)]
    outs = [((T, D), BF), ((2, T, HALF), BF), ((T, D), F32)] + kept
    return pl.pallas_call(
        turn_kernel,
        name="turn",
        out_shape=tuple(jax.ShapeDtypeStruct(s, t) for s, t in outs),
        in_specs=[VM, VM, VM, ANY, VM],
        out_specs=(VM, VM, VM, ANY, ANY, ANY, ANY),
        scratch_shapes=REAR_SCRATCH
        + [pltpu.VMEM(s, t) for s, t in kept]
        + [pltpu.SemaphoreType.DMA((20,))],
        compiler_params=local_params(),
    )(x, mixed, e, w, par)


def back_back_kernel(
    gp, gmid_in, x, stream, middle, pre_in, w, par,
    e, gmixed, gmiddle, sums, mlow_out, gpre_out,
    wo, wf, wp, sems, wq, qsems, res, ssem, rsem, pre, mlow, gpre, psem, osems,
):
    block, partner = partner_of()
    fetch_q = Fetch(w, qsems, QKV_PARTS(wq))
    fetch = Fetch(w, sems, backward_parts(wo, wf, wp))
    load = pltpu.make_async_copy(pre_in, pre, psem)
    load.start()
    greet([partner])

    def hand(i):
        rows = pl.ds(256 * i, 256)
        return remote(res.at[rows], e.at[rows], ssem.at[i], rsem.at[i], partner)

    for k in range(3):
        fetch_q.need(k)

    @pl.when(block == 1)
    def _():
        for i, at in enumerate(TILES):
            front_back_tile(at, nothing, gp, gmid_in, x, wq, par, res, None)
            hand(i).start()
        e[...] = stream[...]

    for k in range(9):
        fetch.need(k)
    load.wait()
    store = Store(osems)

    def put(n, at, cols):
        rows = pl.ds(at.start, at.stop - at.start)
        if cols is None:
            store.put(mlow.at[rows], mlow_out.at[rows])
        else:
            lanes = pl.ds(cols.start, D)
            store.put(gpre.at[rows, lanes], gpre_out.at[rows, lanes])

    for i, at in enumerate(TILES):
        pl.when(block == 0)(hand(i).wait_recv)
        rear_back_tile(
            at, nothing, e, middle, pre, wo, wf, wp, par, gmixed, gmiddle,
            (adder(sums, i), mlow, gpre, put),
        )

    @pl.when(block == 1)
    def _():
        for i in range(2):
            hand(i).wait_send()

    store.finish()


def back_back(gp, gmid, x, stream, middle, pre, w, par):
    dma = pltpu.SemaphoreType.DMA
    return pl.pallas_call(
        back_back_kernel,
        name="front_back_hand_rear_back",
        out_shape=(
            jax.ShapeDtypeStruct((T, D), BF),
            jax.ShapeDtypeStruct((2, T, HALF), BF),
            jax.ShapeDtypeStruct((T, D), F32),
            jax.ShapeDtypeStruct((8, D), F32),
            jax.ShapeDtypeStruct((T, D), BF),
            jax.ShapeDtypeStruct((T, 4 * D), BF),
        ),
        in_specs=[VM, VM, VM, VM, VM, ANY, ANY, VM],
        out_specs=(VM, VM, VM, VM, ANY, ANY),
        scratch_shapes=REAR_SCRATCH
        + [wide(3, 16, 48), dma((3,)), wide(T), dma((2,)), dma((2,))]
        + [pltpu.VMEM((T, 4 * D), BF), wide(T), pltpu.VMEM((T, 4 * D), BF)]
        + [dma, dma((10,))],
        compiler_params=comm_params(4),
    )(gp, gmid, x, stream, middle, pre, w, par)


def front_back_kernel(gp, gmiddle, x, w, par, grad, sums, wq, sems):
    fetch = Fetch(w, sems, QKV_PARTS(wq))
    sums[5:8] = jnp.zeros((3, D), F32)
    for i, at in enumerate(TILES):
        front_back_tile(
            at, nothing if i else fetch.need, gp, gmiddle, x, wq, par, grad, adder(sums, i)
        )


def packed_pieces(gp, at=slice(None)):
    return (
        gp[0, at, :D],
        jnp.concatenate([gp[0, at, D:], gp[1, at, :HALF]], axis=1),
        gp[1, at, HALF:],
    )


def front_back(gp, gmiddle, x, w, par):
    return pl.pallas_call(
        front_back_kernel,
        name="front_back",
        out_shape=(
            jax.ShapeDtypeStruct((T, D), BF),
            jax.ShapeDtypeStruct((8, D), F32),
        ),
        in_specs=[VM, VM, VM, ANY, VM],
        out_specs=(VM, VM),
        scratch_shapes=[wide(3, 16, 48), pltpu.SemaphoreType.DMA((3,))],
        compiler_params=local_params(),
    )(gp, gmiddle, x, w, par)


def weight_grads_kernel(normed, gp, mixed, mlow, normed2, gpre, active, top, small, out):
    def put(m, value):
        at = FC_ROWS[m - 4] if m > 3 else m * 48
        out[:, at : at + 48, :] = value.astype(BF).reshape(16, 48, D)

    for m, piece in enumerate(packed_pieces(gp)):
        put(m, dot_tn(normed[...], piece))
    put(3, dot_tn(jnp.concatenate([mixed[0], mixed[1]], axis=1), mlow[...]))
    for m in range(4):
        put(4 + m, dot_tn(normed2[...], gpre[:, m * D : (m + 1) * D]))
    for m in range(4):
        value = dot_tn(active[:, m * D : (m + 1) * D], top[...])
        out[4 * m : 4 * m + 4, 400:592, :] = value.astype(BF).reshape(4, 192, D)
    out[:, 288:304, :] = small[...]
    out[:, 592:608, :] = jnp.zeros((16, 16, D), BF)


def weight_grads(*operands):
    return pl.pallas_call(
        weight_grads_kernel,
        name="weight_grads",
        out_shape=jax.ShapeDtypeStruct((16, ROWS, D), BF),
        in_specs=[VM] * len(operands),
        out_specs=VM,
        compiler_params=local_params(),
    )(*operands)


STAGES = ((0, 48), (48, 48), (96, 48), (144, 48), (192, 48), (240, 64))


def reduce_kernel(
    grads, result, ingrad, gq, go, gf, gp, gsmall, out_a, out_b,
    own, r0, r1, r2, s1, s2, r3, lsem, s0s, s0r, s1s, s1r, s2s, s2r, s3s, s3r, os, orr, ol,
):
    core, z, y, x = where_am_i()
    block = z % 2
    sib = 1 - core
    dp = y * 4 + x
    sibling = (sib, z, dp)
    first = core == 0
    line = jnp.where(first, y, x)
    place = jnp.where(first, x, y)
    seq = z // 2

    def on_line(step):
        to = (line + step) % 4
        return (core, z, jnp.where(first, to * 4 + x, y * 4 + to))

    def on_place(step):
        to = (place + step) % 4
        return (core, z, jnp.where(first, y * 4 + to, to * 4 + x))

    peers = [sibling]
    for step in (1, 2, 3):
        peers += [on_line(step), on_place(step)]
        for k in (0, 1):
            peers.append((k, (z + step) % 4, dp))
    greet(peers)

    def rows(p):
        return pl.ds(*STAGES[p])

    def span(p, whose):
        at, n = STAGES[p]
        return pl.ds(pl.multiple_of(whose * HROWS + at, 16), n)

    def exchange(p, k):
        return remote(
            own.at[k, :, rows(p)], r0.at[k, :, rows(p)], s0s.at[p, k], s0r.at[p, k], sibling
        )

    def load(p, k):
        return pltpu.make_async_copy(
            r0.at[k, :, rows(p)], own.at[k, :, rows(p)], lsem.at[p, k]
        )

    @pl.when(first)
    def _():
        for p in range(len(STAGES)):
            for k in range(4):
                remote(
                    grads.at[:, k, span(p, sib)],
                    r0.at[k, :, rows(p)],
                    s0s.at[p, k],
                    s0r.at[p, k],
                    sibling,
                ).start()
                pltpu.make_async_copy(
                    grads.at[k, :, span(p, core)], own.at[k, :, rows(p)], lsem.at[p, k]
                ).start()

    @pl.when(jnp.logical_not(first))
    def _():
        for p in range(len(STAGES)):
            for k in range(4):
                remote(
                    grads.at[k, :, span(p, sib)],
                    r0.at[k, :, rows(p)],
                    s0s.at[p, k],
                    s0r.at[p, k],
                    sibling,
                ).start()
                pltpu.make_async_copy(
                    grads.at[:, k, span(p, core)], own.at[k, :, rows(p)], lsem.at[p, k]
                ).start()

    def outputs(j, n):
        src, dst = ((result, out_a), (ingrad, out_b))[n]
        here = (core == block) & (z == 2 * core + j)
        view = src.at[pl.ds(256 * j, 256)]
        keep = pltpu.make_async_copy(view, dst.at[seq], ol.at[n])
        give = remote(
            view, dst.at[seq], os.at[2 * j + n], orr.at[seq, n], (block, 2 * core + j, dp)
        )
        return here, keep, give

    for j in (0, 1):
        for n in (0, 1):
            here, keep, give = outputs(j, n)
            pl.when(here)(keep.start)
            pl.when(jnp.logical_not(here))(give.start)

    def swap_cores(p):
        for k in range(4):
            load(p, k).wait()
            exchange(p, k).wait()

        @pl.loop(0, 16)
        def _(i):
            a = own[i // 4, i % 4, rows(p)].astype(F32)
            b = r0[i // 4, i % 4, rows(p)].astype(F32)
            own[i // 4, i % 4, rows(p)] = (a + b).astype(BF)

        for step in (2, 1, 3):
            remote(
                own.at[(line + step) % 4, :, rows(p)],
                r1.at[step - 1, :, rows(p)],
                s1s.at[p, step],
                s1r.at[p, step],
                on_line(step),
            ).start()

    def over_lines(p):
        for step in (1, 3, 2):
            remote(
                own.at[0, :, rows(p)],
                r1.at[step - 1, :, rows(p)],
                s1s.at[p, step],
                s1r.at[p, step],
                sibling,
            ).wait()

        @pl.loop(0, 4)
        def _(i):
            s1[i, rows(p)] = (
                (own[line, i, rows(p)].astype(F32) + r1[0, i, rows(p)].astype(F32))
                + (r1[1, i, rows(p)].astype(F32) + r1[2, i, rows(p)].astype(F32))
            ).astype(BF)

        for step in (2, 1, 3):
            remote(
                s1.at[(place + step) % 4, rows(p)],
                r2.at[step - 1, rows(p)],
                s2s.at[p, step],
                s2r.at[p, step],
                on_place(step),
            ).start()

    def along_z(p, step):
        return remote(
            s2.at[rows(p)],
            r3.at[core, seq, rows(p)],
            s3s.at[p, step],
            s3r.at[p, core, seq],
            (block, (z + step) % 4, dp),
        )

    def keep_sum(p):
        return pltpu.make_async_copy(s2.at[rows(p)], r3.at[core, seq, rows(p)], ol.at[2 + p])

    def over_places(p):
        for step in (1, 3, 2):
            remote(
                s1.at[0, rows(p)],
                r2.at[step - 1, rows(p)],
                s2s.at[p, step],
                s2r.at[p, step],
                sibling,
            ).wait()
        s2[rows(p)] = (
            (s1[place, rows(p)].astype(F32) + r2[0, rows(p)].astype(F32))
            + (r2[1, rows(p)].astype(F32) + r2[2, rows(p)].astype(F32))
        ).astype(BF)
        for step in (2, 1, 3):
            along_z(p, step).start()
        pl.when(core == block)(keep_sum(p).start)

        @pl.when(core != block)
        def _():
            remote(
                s2.at[rows(p)],
                r3.at[core, seq, rows(p)],
                s3s.at[p, 0],
                s3r.at[p, core, seq],
                sibling,
            ).start()

    def finish(p):
        for step in (1, 2, 3):
            along_z(p, step).wait_send()
        pl.when(core == block)(keep_sum(p).wait)

        @pl.when(core != block)
        def _():
            remote(
                s2.at[rows(p)], s2.at[rows(p)], s3s.at[p, 0], s3r.at[p, 0, 0], sibling
            ).wait_send()

        for c in (0, 1):
            for s in (0, 1):
                here = (core == block) & (core == c) & (seq == s)

                @pl.when(jnp.logical_not(here))
                def _():
                    land = r3.at[c, s, rows(p)]
                    remote(land, land, s3s.at[p, 0], s3r.at[p, c, s], sibling).wait_recv()

        for c in (0, 1):
            at = STAGES[p][0]
            value = r3[c, 0, at : at + 48].astype(F32) + r3[c, 1, at : at + 48].astype(F32)
            if c == 0 and p < 3:
                for side in (0, 1):
                    h, k = (2 * p + side) // 3, (2 * p + side) % 3
                    cols = slice(k * D + h * HALF, k * D + (h + 1) * HALF)
                    gq[0, :, cols] = value[:, side * HALF : (side + 1) * HALF]
            elif c == 0 and p == 3:
                go[0] = value
            elif c == 0:
                gf[0, :, (p - 4) * D : (p - 3) * D] = value
            elif p < 2:
                gf[0, :, (p + 2) * D : (p + 3) * D] = value
            else:
                gp[0, (p - 2) * 48 : (p - 1) * 48] = value
        if p == 5:
            gsmall[...] = r3[0, 0, 288:304].astype(F32) + r3[0, 1, 288:304].astype(F32)

    count = len(STAGES)
    for t in range(count + 3):
        if t < count:
            swap_cores(t)
        if 0 <= t - 1 < count:
            over_lines(t - 1)
        if 0 <= t - 2 < count:
            over_places(t - 2)
        if 0 <= t - 3 < count:
            finish(t - 3)

    for j in (0, 1):
        for n in (0, 1):
            here, keep, give = outputs(j, n)
            pl.when(here)(keep.wait)
            pl.when(jnp.logical_not(here))(give.wait_send)

    for s in (0, 1):
        for n, dst in enumerate((out_a, out_b)):
            here = (core == seq) & (z == 2 * s + core)

            @pl.when(jnp.logical_not(here))
            def _():
                remote(
                    dst.at[s], dst.at[s], os.at[0], orr.at[s, n], sibling
                ).wait_recv()


def reduce(grads, result, ingrad):
    dma = pltpu.SemaphoreType.DMA
    n = len(STAGES)
    return pl.pallas_call(
        reduce_kernel,
        name="reduce_grads",
        out_shape=(
            jax.ShapeDtypeStruct((1, 48, 3 * D), F32),
            jax.ShapeDtypeStruct((1, 48, D), F32),
            jax.ShapeDtypeStruct((1, 48, 4 * D), F32),
            jax.ShapeDtypeStruct((1, 192, D), F32),
            jax.ShapeDtypeStruct((16, D), F32),
            jax.ShapeDtypeStruct((2, 256, D), BF),
            jax.ShapeDtypeStruct((2, 256, D), BF),
        ),
        in_specs=[ANY] + [VM] * 2,
        out_specs=(VM, VM, VM, VM, VM, VM, VM),
        scratch_shapes=[
            pltpu.VMEM((4, 4, HROWS, D), BF),
            pltpu.VMEM((4, 4, HROWS, D), BF),
            pltpu.VMEM((3, 4, HROWS, D), BF),
            pltpu.VMEM((3, HROWS, D), BF),
            pltpu.VMEM((4, HROWS, D), BF),
            pltpu.VMEM((HROWS, D), BF),
            pltpu.VMEM((2, 2, HROWS, D), BF),
            dma((n, 4)),
            dma((n, 4)),
            dma((n, 4)),
            dma((n, 4)),
            dma((n, 4)),
            dma((n, 4)),
            dma((n, 4)),
            dma((n, 4)),
            dma((n, 2, 2)),
            dma((4,)),
            dma((2, 2)),
            dma((2 + n,)),
        ],
        compiler_params=comm_params(5),
    )(grads, result, ingrad)


def halves_first(v, rows):
    return v.reshape(rows, 3, 2, HALF).transpose(0, 2, 1, 3).reshape(rows, 3 * D)


def thirds_first(v, rows):
    return v.reshape(rows, 2, 3, HALF).transpose(0, 2, 1, 3).reshape(rows, 3 * D)


def body(inputs, cotangent, w_qkv, w_out, w_fc, w_proj, gains, biases, fc_bias):
    small = jnp.concatenate([gains.reshape(96), biases.reshape(288), fc_bias.reshape(192)])
    small = jnp.pad(small[None], ((0, 15), (0, D - 576)))
    full, stream = gather(w_qkv, w_out, w_fc, w_proj, small, inputs, cotangent)
    full = full.reshape(16, ROWS, D)

    def lanes(v, rows):
        return v.reshape(16, rows, 48).transpose(1, 0, 2).reshape(rows, D)

    values = full[:, 288, :576].astype(F32)
    shifts = lanes(values[:, 96:384], 6)
    packed_shift = jnp.concatenate([shifts[1], jnp.zeros((D,), F32), shifts[2]])
    par = jnp.concatenate(
        [
            lanes(values[:, :96], 2),
            shifts,
            values[:, 384:].reshape(4, D),
            halves_first(packed_shift[None], 1).reshape(3, D),
            jnp.zeros((1, D), F32),
        ],
        0,
    )

    def attention(packed):
        heads = cross(packed, 1).reshape(L, 3 * HALF)
        mixed_heads, logs = attend(heads)
        return cross(mixed_heads.reshape(2, T, HALF), 2), (heads, mixed_heads, logs)

    def attention_back(kept, gmixed):
        heads, mixed_heads, logs = kept
        gheads = cross(gmixed, 2).reshape(L, HALF)
        gpacked = attend_back(heads, mixed_heads, gheads, logs)
        return cross(gpacked.reshape(2, T, 3 * HALF), 1)

    packed, _ = front(stream, full, par)
    mixed, _ = attention(packed)
    x, packed, normed = rear_front(stream, mixed, full, par)
    mixed, kept = attention(packed)
    result, gmixed, gmiddle, middle, normed2, pre, active = turn(x, mixed, stream, full, par)
    gp = attention_back(kept, gmixed)
    e, gmixed, gmiddle, rear_sums, mlow, gpre = back_back(
        gp, gmiddle, x, stream, middle, pre, full, par
    )
    gp = attention_back(kept, gmixed)
    grad, front_sums = front_back(gp, gmiddle, x, full, par)

    def shards(v, rows):
        return v.reshape(rows, 16, 48).transpose(1, 0, 2).reshape(16, rows * 48)

    packed_sums = thirds_first(front_sums[2:5].reshape(1, 3 * D), 1).reshape(3, D)
    small = jnp.concatenate(
        [
            shards(jnp.stack([front_sums[0], rear_sums[1]]), 2),
            shards(
                jnp.stack(
                    [
                        front_sums[1],
                        packed_sums[0],
                        packed_sums[2],
                        rear_sums[3],
                        rear_sums[2],
                        rear_sums[0],
                    ]
                ),
                6,
            ),
            rear_sums[4:8].reshape(16, 192),
        ],
        1,
    ).astype(BF)
    small = jnp.pad(small[:, None, :], ((0, 0), (0, 15), (0, D - 576)))
    grads = weight_grads(normed, gp, mixed, mlow, normed2, gpre, active, e, small)
    gq, go, gf, gd, total, section_out, in_grad = reduce(
        grads.reshape(4, 4, ROWS, D), result, grad
    )
    tail = total[0, :576]
    return (
        section_out[None],
        in_grad[None],
        gq,
        go,
        gf,
        gd,
        tail[:96].reshape(1, 2, 48),
        tail[96:384].reshape(1, 6, 48),
        tail[384:].reshape(1, 192),
    )


def solution(mesh):
    in_specs = (
        P("dp", "seq", None),
        P("dp", "seq", None),
        P("section", "dp", None),
        P("section", "dp", None),
        P("section", "dp", None),
        P("section", "dp", None),
        P("section", None, "dp"),
        P("section", None, "dp"),
        P("section", "dp"),
    )
    out_specs = (
        P("section", "dp", "seq", None),
        P("section", "dp", "seq", None),
        P("section", "dp", None),
        P("section", "dp", None),
        P("section", "dp", None),
        P("section", "dp", None),
        P("section", None, "dp"),
        P("section", None, "dp"),
        P("section", "dp"),
    )
    return jax.shard_map(body, mesh=mesh, in_specs=in_specs, out_specs=out_specs, check_vma=False)
```

time: 641 us -> 358 us (0.56)
  Pallas kernels: 603 us -> 328 us
    pallas_call x8, Pallas kernels: 202 us -> 23.2 us  [cross(): pl.pallas_call(cross_kernel, name='cross_cores', out_shape=jax.ShapeDtype...]
    pallas_call x1, Pallas kernels: 98.5 us -> 55.8 us  [gather(): pl.pallas_call(gather_kernel, name='gather_weights', out_shape=(jax.Shape...]
    pallas_call x1, Pallas kernels: 101 us -> 72.8 us  [reduce(): pl.pallas_call(reduce_kernel, name='reduce_grads', out_shape=(jax.ShapeDt...]
    pallas_call x10 -> x5, Pallas kernels: 126 us -> 101 us  [the longest x1 38.2 us: back_back(): pl.pallas_call(back_back_kernel, name='front_back_hand_rear_back', out_sh...]
where the time goes in v2:
time: 358 us; the launch traced here: 351 us
  Pallas kernels  328 us (92%)
  local copies, waits for them, and re-layouts  17.4 us (5%)
    pallas_call x1, Pallas kernels, reduce(): pl.pallas_call(reduce_kernel, name='reduce_grads', out_shape=(jax.ShapeDt...  72.8 us
    pallas_call x1, Pallas kernels, gather(): pl.pallas_call(gather_kernel, name='gather_weights', out_shape=(jax.Shape...  55.8 us
    pallas_call x1, Pallas kernels, back_back(): pl.pallas_call(back_back_kernel, name='front_back_hand_rear_back', out_sh...  38.2 us
    pallas_call x2, Pallas kernels, attend_back(): pl.pallas_call(attend_back_kernel, name='attend_back', grid=(3,), out_sha...  33.9 us
    pallas_call x1, Pallas kernels, rear_front(): pl.pallas_call(rear_front_kernel, name='rear_hand_front', out_shape=(jax....  26.8 us
    pallas_call x2, Pallas kernels, attend(): pl.pallas_call(attend_kernel, name='attend', grid=(3,), out_shape=(jax.Sh...  24.4 us
    pallas_call x8, Pallas kernels, cross(): pl.pallas_call(cross_kernel, name='cross_cores', out_shape=jax.ShapeDtype...  23.2 us
    pallas_call x1, Pallas kernels, turn(): pl.pallas_call(turn_kernel, name='turn', out_shape=tuple((jax.ShapeDtypeS...  20.8 us

profile of v2, /device:TPU:1, one launch (start us, length us, event | category | flops | bytes accessed | tf_op | source)
XLA Modules:
  0.0 350.6 jit_solution(9349798354432195430)
XLA Ops:
  2.1 0.8 reshape.164
  3.6 55.8 %gather_weights.1 = (bf16[4,4,608,768]{3,2,1,0:T(8,128)(2,1)}, bf16[512,768]{1,0:T(8,128)(2,1)}) custom-call(bf16[1,48,2304]{2,1,0:T(8,128)(2,1)} %wq.1, bf16[1,48,768]{2,1,0:T(8,128)(2,1)} %wo.1, bf16[1,48,3072]{2,1,0:T(8,128)(2,1)} %wf.1, bf16[1,192,768]{2,1,0:T(8,128)(2,1)} %wp.1, bf16[16,768]{1,0:T(8,128)(2,1)} %pad.8.small, bf16[2,256,768]{2,1,0:T(8,128)(2,1)} %ins.1, ...), custom_call_target="tpu_custom_call" | custom-call | tf_op jit(solution)/shard_map/gather_weights/pallas_call | solution.py:234
  59.3 0.9 slice_convert_fusion
  61.1 1.3 concatenate.30.par
  62.4 6.4 %front.1 = (bf16[2,512,1152]{2,1,0:T(8,128)(2,1)}, bf16[512,768]{1,0:T(8,128)(2,1)}) custom-call(bf16[512,768]{1,0:T(8,128)(2,1)} %get-tuple-element.40.x.e.stream, bf16[16,608,768]{2,1,0:T(8,128)(2,1)} %bitcast.26, f32[16,768]{1,0:T(8,128)} %concatenate.30.par), custom_call_target="tpu_custom_call" | custom-call | tf_op jit(solution)/shard_map/front/pallas_call | solution.py:391
  68.8 3.7 %cross_cores.8 = bf16[2,512,1152]{2,1,0:T(8,128)(2,1)} custom-call(bf16[2,512,1152]{2,1,0:T(8,128)(2,1)} %get-tuple-element.42.src), custom_call_target="tpu_custom_call" | custom-call | tf_op jit(solution)/shard_map/cross_cores/pallas_call | solution.py:275
  72.6 12.0 %attend.2 = (bf16[1024,384]{1,0:T(8,128)(2,1)}, f32[3,1024,128]{2,1,0:T(8,128)}) custom-call(bf16[1024,1152]{1,0:T(8,128)(2,1)} %bitcast.41, bf16[1024,1152]{1,0:T(8,128)(2,1)} %bitcast.42, bf16[1024,1152]{1,0:T(8,128)(2,1)} %bitcast.43), custom_call_target="tpu_custom_call" | custom-call | tf_op jit(solution)/shard_map/attend/pallas_call | solution.py:449
  84.5 2.1 cross_cores.9.mixed
  86.6 26.8 %rear_hand_front.1 = (bf16[512,768]{1,0:T(8,128)(2,1)}, bf16[2,512,1152]{2,1,0:T(8,128)(2,1)}, bf16[512,768]{1,0:T(8,128)(2,1)}) custom-call(bf16[512,768]{1,0:T(8,128)(2,1)} %get-tuple-element.40.x.e.stream, bf16[2,512,384]{2,1,0:T(8,128)(2,1)} %cross_cores.9.mixed, bf16[16,608,768]{2,1,0:T(8,128)(2,1)} %bitcast.27, f32[16,768]{1,0:T(8,128)} %concatenate.30.par), custom_call_target="tpu_custom_call" | custom-call | tf_op jit(solution)/shard_map/rear_hand_front/pallas_call | solution.py:691
  113.4 3.8 %cross_cores.10 = bf16[2,512,1152]{2,1,0:T(8,128)(2,1)} custom-call(bf16[2,512,1152]{2,1,0:T(8,128)(2,1)} %get-tuple-element.45.src), custom_call_target="tpu_custom_call" | custom-call | tf_op jit(solution)/shard_map/cross_cores/pallas_call | solution.py:275
  117.2 12.4 %attend.3 = (bf16[1024,384]{1,0:T(8,128)(2,1)}, f32[3,1024,128]{2,1,0:T(8,128)}) custom-call(bf16[1024,1152]{1,0:T(8,128)(2,1)} %bitcast.31, bf16[1024,1152]{1,0:T(8,128)(2,1)} %bitcast.32, bf16[1024,1152]{1,0:T(8,128)(2,1)} %bitcast.33), custom_call_target="tpu_custom_call" | custom-call | tf_op jit(solution)/shard_map/attend/pallas_call | solution.py:449
  129.6 2.2 cross_cores.11.mixed
  131.8 20.8 %turn.1 = (bf16[512,768]{1,0:T(8,128)(2,1)}, bf16[2,512,384]{2,1,0:T(8,128)(2,1)}, f32[512,768]{1,0:T(8,128)}, f32[512,768]{1,0:T(8,128)}, bf16[512,768]{1,0:T(8...) custom-call(bf16[512,768]{1,0:T(8,128)(2,1)} %get-tuple-element.47.x, ...), custom_call_target="tpu_custom_call" | custom-call | tf_op jit(solution)/shard_map/turn/pallas_call | solution.py:736
  152.6 2.2 cross_cores.12
  154.8 16.8 %attend_back.2 = bf16[1024,1152]{1,0:T(8,128)(2,1)} custom-call(bf16[1024,1152]{1,0:T(8,128)(2,1)} %bitcast.34, bf16[1024,1152]{1,0:T(8,128)(2,1)} %bitcast.35, bf16[1024,1152]{1,0:T(8,128)(2,1)} %bitcast.36, bf16[1024,384]{1,0:T(8,128)(2,1)} %get-tuple-element.46.o_ref, bf16[1024,384]{1,0:T(8,128)(2,1)} %bitcast.48, f32[3,1024,128]{2,1,0:T(8,128)} %get-tuple-element.49.logs), custom_call_target="tpu_custom_call" | custom-call | tf_op jit(solution)/shard_map/attend_back/pallas_call | solution.py:502
  171.6 3.2 cross_cores.13.gp
  174.8 38.2 %front_back_hand_rear_back.1 = (bf16[512,768]{1,0:T(8,128)(2,1)}, bf16[2,512,384]{2,1,0:T(8,128)(2,1)}, f32[512,768]{1,0:T(8,128)}, f32[8,768]{1,0:T(8,128)}, bf...) custom-call(bf16[2,512,1152]{2,1,0:T(8,128)(2,1)} %cross_cores.13.gp, f32[512,768]{1,0:T(8,128)} %get-tuple-element.50.gmid_in, ...), custom_call_target="tpu_custom_call" | custom-call | tf_op jit(solution)/shard_map/front_back_hand_rear_back/pallas_call | solution.py:805
  213.1 2.7 cross_cores.14
  215.8 17.1 %attend_back.3 = bf16[1024,1152]{1,0:T(8,128)(2,1)} custom-call(bf16[1024,1152]{1,0:T(8,128)(2,1)} %bitcast.37, bf16[1024,1152]{1,0:T(8,128)(2,1)} %bitcast.38, bf16[1024,1152]{1,0:T(8,128)(2,1)} %bitcast.39, bf16[1024,384]{1,0:T(8,128)(2,1)} %get-tuple-element.46.o_ref, bf16[1024,384]{1,0:T(8,128)(2,1)} %bitcast.47, f32[3,1024,128]{2,1,0:T(8,128)} %get-tuple-element.49.logs), custom_call_target="tpu_custom_call" | custom-call | tf_op jit(solution)/shard_map/attend_back/pallas_call | solution.py:502
  232.8 3.3 cross_cores.15.gp
  236.2 8.7 %front_back.1 = (bf16[512,768]{1,0:T(8,128)(2,1)}, f32[8,768]{1,0:T(8,128)}) custom-call(bf16[2,512,1152]{2,1,0:T(8,128)(2,1)} %cross_cores.15.gp, f32[512,768]{1,0:T(8,128)} %get-tuple-element.59.gmiddle, bf16[512,768]{1,0:T(8,128)(2,1)} %get-tuple-element.47.x, bf16[16,608,768]{2,1,0:T(8,128)(2,1)} %bitcast.30, f32[16,768]{1,0:T(8,128)} %concatenate.30.par), custom_call_target="tpu_custom_call" | custom-call | tf_op jit(solution)/shard_map/front_back/pallas_call | solution.py:844
  247.5 0.9 fusion.8.small
  248.4 17.4 %weight_grads.1 = bf16[16,608,768]{2,1,0:T(8,128)(2,1)} custom-call(bf16[512,768]{1,0:T(8,128)(2,1)} %get-tuple-element.44.normed, bf16[2,512,1152]{2,1,0:T(8,128)(2,1)} %cross_cores.15.gp, bf16[2,512,384]{2,1,0:T(8,128)(2,1)} %cross_cores.11.mixed, bf16[512,768]{1,0:T(8,128)(2,1)} %get-tuple-element.54.mlow, bf16[512,768]{1,0:T(8,128)(2,1)} %get-tuple-element.55.normed2, ...), custom_call_target="tpu_custom_call" | custom-call | tf_op jit(solution)/shard_map/weight_grads/pallas_call | solution.py:876
  265.9 72.8 %reduce_grads.1 = (f32[1,48,2304]{2,1,0:T(8,128)}, f32[1,48,768]{2,1,0:T(8,128)}, f32[1,48,3072]{2,1,0:T(8,128)}, f32[1,192,768]{2,1,0:T(8,128)}, f32[16,768]{1,...) custom-call(bf16[4,4,608,768]{3,2,1,0:T(8,128)(2,1)} %bitcast.40, ...), custom_call_target="tpu_custom_call" | custom-call | tf_op jit(solution)/shard_map/reduce_grads/pallas_call | solution.py:1136
  338.7 0.8 slice_reduce_fusion.9
  340.2 1.3 slice.95
  341.4 0.8 slice_reduce_fusion.8
  342.9 2.1 copy.53
  345.0 2.1 copy.54
  347.1 0.8 copy.55
  348.5 0.8 copy.57
  349.3 0.8 copy.58
  (64 shorter events, 7.5 us)
Async XLA Ops:
  236.2 10.5 %copy-start.4 = (f32[8,768]{1,0:T(8,128)S(1)}, f32[8,768]{1,0:T(8,128)}, u32[]{:S(2)}) copy-start(f32[8,768]{1,0:T(8,128)} %get-tuple-element.61) | copy-start | bytes 73732
  338.7 8.4 %copy-start.2 = (f32[1,48,2304]{2,1,0:T(8,128)S(1)}, f32[1,48,2304]{2,1,0:T(8,128)}, u32[]{:S(2)}) copy-start(f32[1,48,2304]{2,1,0:T(8,128)} %get-tuple-element.112) | copy-start | bytes 1327108
  338.7 9.1 %copy-start.3 = (f32[1,48,768]{2,1,0:T(8,128)S(1)}, f32[1,48,768]{2,1,0:T(8,128)}, u32[]{:S(2)}) copy-start(f32[1,48,768]{2,1,0:T(8,128)} %get-tuple-element.113) | copy-start | bytes 442372
  338.7 9.8 %copy-start.1 = (f32[1,48,3072]{2,1,0:T(8,128)S(1)}, f32[1,48,3072]{2,1,0:T(8,128)}, u32[]{:S(2)}) copy-start(f32[1,48,3072]{2,1,0:T(8,128)} %get-tuple-element.114) | copy-start | bytes 1769476
  345.0 4.4 %copy-start = (f32[1,192,768]{2,1,0:T(8,128)S(1)}, f32[1,192,768]{2,1,0:T(8,128)}, u32[]{:S(2)}) copy-start(f32[1,192,768]{2,1,0:T(8,128)} %get-tuple-element.115) | copy-start | bytes 1769476
